TPU v7x, 1024 devices: a whole 4x4x32 slice. The times are simulated.
1024 devices in a mesh: pp: 16 (over y, x_lo, core), ep: 64 (over x_hi, z).
Axes of the slice: x: 4 (x_hi: 2, x_lo: 2; x = x_hi * 2 + x_lo), y: 4, z: 32, core: 2. Of those that a mesh axis runs over, the one named last changes fastest.
Arguments:
- forward_input_rows: bfloat16 [16, 2048, 7168], P('pp', 'ep'), may hold values from -6 to 6
- ids_fwd: int32 [16, 2048, 8], P('pp', 'ep'), may hold values from 0 to 255, as said below
- gate_fwd: float32 [16, 2048, 8], P('pp', 'ep'), may hold values from 0.1 to 1
- backward_input_rows: bfloat16 [16, 2048, 7168], P('pp', 'ep'), may hold values from -6 to 6
- dy_bwd: bfloat16 [16, 2048, 7168], P('pp', 'ep'), may hold values from -6 to 6
- ids_bwd: int32 [16, 2048, 8], P('pp', 'ep'), may hold values from 0 to 255, as said below
- gate_bwd: float32 [16, 2048, 8], P('pp', 'ep'), may hold values from 0.1 to 1
- saved_z: bfloat16 [16, 2, 8192, 128], P('pp', None, 'ep'), may hold values from -8 to 8
- norm_gain: float32 [16, 7168], P('pp'), may hold values from 0.25 to 1.75
- w_gate: bfloat16 [7168, 8192], P(None, 'ep'), may hold values from -0.0625 to 0.0625
- w_up: bfloat16 [7168, 8192], P(None, 'ep'), may hold values from -0.0625 to 0.0625
- w_down: bfloat16 [8192, 7168], P('ep'), may hold values from -0.125 to 0.125
Outputs:
- y_fwd: bfloat16 [16, 2048, 7168], P('pp', 'ep')
- grad_x_bwd: bfloat16 [16, 2048, 7168], P('pp', 'ep')
- grad_gate_bwd: float32 [16, 2048, 8], P('pp', 'ep')
- grad_gain: float32 [16, 64, 7168], P('pp', 'ep')
Inputs may be any that keep to these rules, and one draw needn't show every extreme that they name: `ids_fwd`: each token names 8 different experts; at most one of them is below 4. Among the 32 tokens of one device at most 2 name any one expert below 4, and in every draw some expert below 4 is named by exactly 2 tokens of every device. `ids_bwd`: as for ids_fwd.
All inputs are finite; a program needn't handle non-finite values.
Results may differ from a plain program's by a relative error of at most 0.0085.
Values may be sent and summed in bfloat16 or wider, within the bound.
A program may use at most 64 MiB of HBM per device.

v0:
```python
import jax
import jax.numpy as jnp
from jax import lax
from jax.sharding import PartitionSpec as P

CAP = 2


EPSILON = 1e-06


def from_partner(value, axis, stride):
    mask = 2**stride
    pairs = [(source, source ^ mask) for source in range(lax.axis_size(axis))]
    return lax.ppermute(value, axis, pairs)


def route_tables(id_rows, gate_rows, experts):
    tokens = id_rows.shape[0]
    window = id_rows < experts
    labels = jnp.arange(experts, dtype=jnp.int32)
    hit_table = jnp.any(id_rows[:, :, None] == labels[None, None, :], axis=1).astype(jnp.float32)
    earlier = (jnp.arange(tokens)[:, None] > jnp.arange(tokens)[None, :]).astype(jnp.float32)
    slot_rank = jnp.dot(earlier, hit_table, precision=lax.Precision.HIGHEST)
    slot_ids = jnp.arange(CAP, dtype=jnp.float32)
    select = hit_table.T[:, None, :] * (slot_rank.T[:, None, :] == slot_ids[None, :, None]).astype(
        jnp.float32
    )
    pick_gate = jnp.sum(jnp.where(window, gate_rows, 0.0), axis=1)
    return (select, pick_gate, window)


def row_norm_values(x_rows):
    x_float = x_rows.astype(jnp.float32)
    inverse_root_scale = lax.rsqrt(jnp.mean(x_float * x_float, axis=-1, keepdims=True) + EPSILON)
    return (x_float * inverse_root_scale, inverse_root_scale)


def pack_rows(select, values, split_count):
    packed = jnp.einsum(
        "ejt,td->ejd", select.astype(jnp.bfloat16), values, preferred_element_type=jnp.float32
    ).astype(jnp.bfloat16)
    experts, slots, width = packed.shape
    spread = jnp.broadcast_to(packed[:, None], (experts, split_count, slots, width))
    return spread.reshape(experts * split_count, slots, width)


def fold_slices(returned, experts, split_count):
    return jnp.sum(
        returned.reshape((experts, split_count) + returned.shape[1:]).astype(jnp.float32), axis=1
    )


def to_tokens(select, per_slot):
    return jnp.einsum("ejt,ejd->td", select, per_slot, precision=lax.Precision.HIGHEST)


def transposed_dot(left, right):
    return lax.dot_general(
        left, right, (((1,), (1,)), ((), ())), preferred_element_type=jnp.float32
    )


def per_device(
    forward_input_rows,
    ids_fwd,
    gate_fwd,
    backward_input_rows,
    dy_bwd,
    ids_bwd,
    gate_bwd,
    saved_z,
    norm_gain,
    w_gate,
    w_up,
    w_down,
):
    ep_count = lax.axis_size("ep")
    split_count = min(16, ep_count)
    experts = ep_count // split_count
    gain_vector_row = norm_gain[0]
    width = forward_input_rows.shape[2]
    select, pick_gate, window = route_tables(ids_fwd[0], gate_fwd[0], experts)
    centered_input_estimate, inverse_root_scale = row_norm_values(forward_input_rows[0])
    normalized_output = (centered_input_estimate * gain_vector_row).astype(jnp.bfloat16)
    outgoing = pack_rows(select, normalized_output, split_count)
    received = lax.all_to_all(outgoing, "ep", split_axis=0, concat_axis=0, tiled=True)
    flat_rows = received.reshape(-1, width)
    z_gate = jnp.dot(flat_rows, w_gate, preferred_element_type=jnp.float32)
    z_up = jnp.dot(flat_rows, w_up, preferred_element_type=jnp.float32)
    activation = (jax.nn.silu(z_gate) * z_up).astype(jnp.bfloat16)
    partial_value = jnp.dot(activation, w_down, preferred_element_type=jnp.float32).astype(
        jnp.bfloat16
    )
    returned = lax.all_to_all(
        partial_value.reshape(received.shape), "ep", split_axis=0, concat_axis=0, tiled=True
    )
    per_slot = fold_slices(returned, experts, split_count)
    mixed_rows = pick_gate[:, None] * to_tokens(select, per_slot)
    y_rows = mixed_rows.astype(jnp.bfloat16)[None]
    select, pick_gate, window = route_tables(ids_bwd[0], gate_bwd[0], experts)
    outgoing = pack_rows(select, dy_bwd[0], split_count)
    received = lax.all_to_all(outgoing, "ep", split_axis=0, concat_axis=0, tiled=True)
    flat_rows = received.reshape(-1, width)
    grad_act = transposed_dot(flat_rows, w_down)
    pre_gate = saved_z[0, 0].astype(jnp.float32)
    pre_up = saved_z[0, 1].astype(jnp.float32)
    sigmoid_gate = jax.nn.sigmoid(pre_gate)
    silu_gate = pre_gate * sigmoid_gate
    activation = lax.optimization_barrier((silu_gate * pre_up).astype(jnp.bfloat16)).astype(
        jnp.float32
    )
    grad_gate = (grad_act * pre_up * sigmoid_gate * (1.0 + pre_gate * (1.0 - sigmoid_gate))).astype(
        jnp.bfloat16
    )
    grad_up = (grad_act * silu_gate).astype(jnp.bfloat16)
    partial_value = (transposed_dot(grad_gate, w_gate) + transposed_dot(grad_up, w_up)).astype(
        jnp.bfloat16
    )
    slot_score = (
        jnp.sum(grad_act * activation, axis=1).reshape(received.shape[:2]).astype(jnp.bfloat16)
    )
    back_part = lax.all_to_all(
        partial_value.reshape(received.shape), "ep", split_axis=0, concat_axis=0, tiled=True
    )
    back_score = lax.all_to_all(slot_score, "ep", split_axis=0, concat_axis=0, tiled=True)
    gradient_normalized_rows = pick_gate[:, None] * to_tokens(
        select, fold_slices(back_part, experts, split_count)
    )
    score_slots = fold_slices(back_score, experts, split_count)
    token_score = jnp.einsum("ejt,ej->t", select, score_slots, precision=lax.Precision.HIGHEST)
    grad_gate_out = jnp.where(window, token_score[:, None], 0.0)
    centered_input_estimate, inverse_root_scale = row_norm_values(backward_input_rows[0])
    gain_product_term = jnp.sum(gradient_normalized_rows * centered_input_estimate, axis=0)
    scaled_rows = gradient_normalized_rows * gain_vector_row
    input_gradient = inverse_root_scale * (
        scaled_rows
        - centered_input_estimate
        * jnp.mean(scaled_rows * centered_input_estimate, axis=-1, keepdims=True)
    )
    grad_rows, grad_picks, gain_product_term = (
        input_gradient.astype(jnp.bfloat16)[None],
        grad_gate_out[None],
        gain_product_term,
    )
    mirrored = gain_product_term
    for bit_index in range(lax.axis_size("pp").bit_length() - 1):
        mirrored = from_partner(mirrored, "pp", bit_index)
    grad_gain = (gain_product_term + mirrored)[None, None]
    return (y_rows, grad_rows, grad_picks, grad_gain)


def solution(mesh):
    placed = (
        P("pp", "ep", None),
        P("pp", "ep", None),
        P("pp", "ep", None),
        P("pp", "ep", None),
        P("pp", "ep", None),
        P("pp", "ep", None),
        P("pp", "ep", None),
        P("pp", None, "ep", None),
        P("pp", None),
        P(None, "ep"),
        P(None, "ep"),
        P("ep", None),
    )
    return jax.shard_map(
        per_device,
        mesh=mesh,
        in_specs=placed,
        out_specs=(
            P("pp", "ep", None),
            P("pp", "ep", None),
            P("pp", "ep", None),
            P("pp", "ep", None),
        ),
        check_vma=False,
    )
```

profile of v0, /device:TPU:96, one launch (start us, length us, event | category | flops | bytes accessed | tf_op | source)
XLA Modules:
  0.0 805.3 jit_solution(16295744460962412289)
XLA Ops:
  0.6 0.8 fusion.51
  1.5 0.1 fusion.48
  1.6 1.2 convolution_convert_fusion.1
  2.8 0.1 copy.54
  2.9 2.2 broadcast_in_dim.26
  5.1 30.9 %all-to-all-start.2 = ((bf16[64,2,7168]{2,1,0:T(2,128)(2,1)}), bf16[64,2,7168]{2,1,0:T(2,128)(2,1)}, u32[]{:S(2)}, u32[]{:S(2)}) async-start(bf16[64,2,7168]{2,1,0:T(2,128)(2,1)} %bitcast.101), calls=%async_computation.2 | async-start | bytes 3670016 | tf_op jit(solution)/shard_map/all_to_all | solution.py:103
  36.0 0.2 fusion.9
  36.2 0.1 fusion.49
  36.4 0.3 convolution_convert_fusion.2
  36.7 0.1 copy.52
  36.8 173.7 %all-to-all-done.2 = bf16[64,2,7168]{2,1,0:T(2,128)(2,1)} async-done(((bf16[64,2,7168]{2,1,0:T(2,128)(2,1)}), bf16[64,2,7168]{2,1,0:T(2,128)(2,1)}, u32[]{:S(2)}, u32[]{:S(2)}) %all-to-all-start.2) | async-done | bytes 1835040 | tf_op jit(solution)/shard_map/all_to_all | solution.py:103
  210.5 2.2 broadcast_in_dim.24
  212.7 8.4 %all-to-all-start = ((bf16[64,2,7168]{2,1,0:T(2,128)(2,1)}), bf16[64,2,7168]{2,1,0:T(2,128)(2,1)}, u32[]{:S(2)}, u32[]{:S(2)}) async-start(bf16[64,2,7168]{2,1,0:T(2,128)(2,1)} %bitcast.100), calls=%async_computation | async-start | bytes 3670016 | tf_op jit(solution)/shard_map/all_to_all | solution.py:87
  221.2 4.9 reshape.98
  226.1 2.8 multiply_reduce_fusion
  228.9 0.8 convert_element_type.161
  229.7 3.9 fusion.40
  233.6 162.1 %all-to-all-done = bf16[64,2,7168]{2,1,0:T(2,128)(2,1)} async-done(((bf16[64,2,7168]{2,1,0:T(2,128)(2,1)}), bf16[64,2,7168]{2,1,0:T(2,128)(2,1)}, u32[]{:S(2)}, u32[]{:S(2)}) %all-to-all-start) | async-done | bytes 1835040 | tf_op jit(solution)/shard_map/all_to_all | solution.py:87
  395.7 8.1 %all-to-all-start.4 = ((bf16[64,1,2]{2,1,0:T(2,128)(2,1)}), bf16[64,1,2]{2,1,0:T(2,128)(2,1)S(1)}, u32[]{:S(2)}, u32[]{:S(2)}) async-start(bf16[64,1,2]{2,1,0:T(2,128)(2,1)} %convert_element_type.161), calls=%async_computation.4 | async-start | bytes 65536 | tf_op jit(solution)/shard_map/all_to_all | solution.py:126
  403.8 4.0 fusion
  407.8 4.7 reshape.99
  412.5 13.5 %all-to-all-done.4 = bf16[64,1,2]{2,1,0:T(2,128)(2,1)S(1)} async-done(((bf16[64,1,2]{2,1,0:T(2,128)(2,1)}), bf16[64,1,2]{2,1,0:T(2,128)(2,1)S(1)}, u32[]{:S(2)}, u32[]{:S(2)}) %all-to-all-start.4) | async-done | bytes 288 | tf_op jit(solution)/shard_map/all_to_all | solution.py:126
  426.1 11.4 %all-to-all-start.3 = ((bf16[64,2,7168]{2,1,0:T(2,128)(2,1)}), bf16[64,2,7168]{2,1,0:T(2,128)(2,1)}, u32[]{:S(2)}, u32[]{:S(2)}) async-start(bf16[64,2,7168]{2,1,0:T(2,128)(2,1)} %reshape.99), calls=%async_computation.3 | async-start | bytes 3670016 | tf_op jit(solution)/shard_map/all_to_all | solution.py:123
  437.5 4.9 reshape.95
  442.5 2.7 fusion.80
  445.1 4.6 convolution_convert_fusion
  449.7 4.8 reshape.96
  454.5 157.0 %all-to-all-done.3 = bf16[64,2,7168]{2,1,0:T(2,128)(2,1)} async-done(((bf16[64,2,7168]{2,1,0:T(2,128)(2,1)}), bf16[64,2,7168]{2,1,0:T(2,128)(2,1)}, u32[]{:S(2)}, u32[]{:S(2)}) %all-to-all-start.3) | async-done | bytes 1835040 | tf_op jit(solution)/shard_map/all_to_all | solution.py:123
  611.5 8.3 %all-to-all-start.1 = ((bf16[64,2,7168]{2,1,0:T(2,128)(2,1)}), bf16[64,2,7168]{2,1,0:T(2,128)(2,1)}, u32[]{:S(2)}, u32[]{:S(2)}) async-start(bf16[64,2,7168]{2,1,0:T(2,128)(2,1)} %reshape.96), calls=%async_computation.1 | async-start | bytes 3670016 | tf_op jit(solution)/shard_map/all_to_all | solution.py:95
  619.9 0.2 fusion.17
  620.1 0.1 copy.60
  620.3 0.1 reduce_sum.98
  620.4 0.2 convolution_bitcast_fusion.2
  620.6 0.6 compare_select_fusion
  621.2 3.1 convert_reduce_fusion
  624.3 1.3 fusion.16
  625.6 1.9 collective-permute-start
  627.5 1.2 collective-permute-done
  628.7 2.5 collective-permute-start.1
  631.2 1.0 fusion.18
  632.2 2.5 collective-permute-done.1
  634.7 3.5 collective-permute-start.2
  638.2 156.1 %all-to-all-done.1 = bf16[64,2,7168]{2,1,0:T(2,128)(2,1)} async-done(((bf16[64,2,7168]{2,1,0:T(2,128)(2,1)}), bf16[64,2,7168]{2,1,0:T(2,128)(2,1)}, u32[]{:S(2)}, u32[]{:S(2)}) %all-to-all-start.1) | async-done | bytes 1835040 | tf_op jit(solution)/shard_map/all_to_all | solution.py:95
  794.3 3.1 convert_reduce_fusion.1
  797.4 5.1 collective-permute-start.3
  802.6 1.7 fusion.4
  804.3 0.4 collective-permute-done.3
  804.7 0.6 add.38
  (29 shorter events, 0.3 us)
Async XLA Ops:
  0.6 403.2 %copy-start = (bf16[7168,128]{1,0:T(8,128)(2,1)S(1)}, bf16[7168,128]{1,0:T(8,128)(2,1)}, u32[]{:S(2)}) copy-start(bf16[7168,128]{1,0:T(8,128)(2,1)} %param.22) | copy-start | bytes 5505028
  5.1 30.9 %copy-start.6 = (s32[1,32,8]{1,2,0:T(8,128)S(1)}, s32[1,32,8]{1,2,0:T(8,128)}, u32[]{:S(2)}) copy-start(s32[1,32,8]{1,2,0:T(8,128)} %param.13) | copy-start | bytes 3076
  5.1 30.9 %copy-start.2 = (bf16[1,32,7168]{2,1,0:T(8,128)(2,1)S(1)}, bf16[1,32,7168]{2,1,0:T(8,128)(2,1)}, u32[]{:S(2)}) copy-start(bf16[1,32,7168]{2,1,0:T(8,128)(2,1)} %param.12) | copy-start | bytes 1376260
  5.1 31.3 %copy-start.5 = (f32[1,7168]{1,0:T(1,128)S(1)}, f32[1,7168]{1,0:T(1,128)}, u32[]{:S(2)}) copy-start(f32[1,7168]{1,0:T(1,128)} %param.20) | copy-start | bytes 86020
  5.1 205.4 %all-to-all-start.2 = ((bf16[64,2,7168]{2,1,0:T(2,128)(2,1)}), bf16[64,2,7168]{2,1,0:T(2,128)(2,1)}, u32[]{:S(2)}, u32[]{:S(2)}) async-start(bf16[64,2,7168]{2,1,0:T(2,128)(2,1)} %bitcast.101), calls=%async_computation.2 | async-start | bytes 3670016 | tf_op jit(solution)/shard_map/all_to_all | solution.py:103
  212.7 8.4 %copy-start.3 = (bf16[1,2,128,128]{3,2,1,0:T(8,128)(2,1)S(1)}, bf16[1,2,128,128]{3,2,1,0:T(8,128)(2,1)}, u32[]{:S(2)}) copy-start(bf16[1,2,128,128]{3,2,1,0:T(8,128)(2,1)} %param.19) | copy-start | bytes 196612
  212.7 183.0 %all-to-all-start = ((bf16[64,2,7168]{2,1,0:T(2,128)(2,1)}), bf16[64,2,7168]{2,1,0:T(2,128)(2,1)}, u32[]{:S(2)}, u32[]{:S(2)}) async-start(bf16[64,2,7168]{2,1,0:T(2,128)(2,1)} %bitcast.100), calls=%async_computation | async-start | bytes 3670016 | tf_op jit(solution)/shard_map/all_to_all | solution.py:87
  395.7 30.4 %all-to-all-start.4 = ((bf16[64,1,2]{2,1,0:T(2,128)(2,1)}), bf16[64,1,2]{2,1,0:T(2,128)(2,1)S(1)}, u32[]{:S(2)}, u32[]{:S(2)}) async-start(bf16[64,1,2]{2,1,0:T(2,128)(2,1)} %convert_element_type.161), calls=%async_computation.4 | async-start | bytes 65536 | tf_op jit(solution)/shard_map/all_to_all | solution.py:126
  426.1 185.4 %all-to-all-start.3 = ((bf16[64,2,7168]{2,1,0:T(2,128)(2,1)}), bf16[64,2,7168]{2,1,0:T(2,128)(2,1)}, u32[]{:S(2)}, u32[]{:S(2)}) async-start(bf16[64,2,7168]{2,1,0:T(2,128)(2,1)} %reshape.99), calls=%async_computation.3 | async-start | bytes 3670016 | tf_op jit(solution)/shard_map/all_to_all | solution.py:123
  454.5 165.3 %copy-start.4 = (s32[1,32,8]{1,2,0:T(8,128)S(1)}, s32[1,32,8]{1,2,0:T(8,128)}, u32[]{:S(2)}) copy-start(s32[1,32,8]{1,2,0:T(8,128)} %param.17) | copy-start | bytes 3076
  454.5 165.3 %copy-start.7 = (f32[1,32,8]{1,2,0:T(8,128)S(1)}, f32[1,32,8]{1,2,0:T(8,128)}, u32[]{:S(2)}) copy-start(f32[1,32,8]{1,2,0:T(8,128)} %param.18) | copy-start | bytes 3076
  454.5 165.3 %copy-start.8 = (f32[1,32,8]{1,2,0:T(8,128)S(1)}, f32[1,32,8]{1,2,0:T(8,128)}, u32[]{:S(2)}) copy-start(f32[1,32,8]{1,2,0:T(8,128)} %param.14) | copy-start | bytes 3076
  454.5 165.4 %copy-start.1 = (bf16[1,32,7168]{2,1,0:T(8,128)(2,1)S(1)}, bf16[1,32,7168]{2,1,0:T(8,128)(2,1)}, u32[]{:S(2)}) copy-start(bf16[1,32,7168]{2,1,0:T(8,128)(2,1)} %param.15) | copy-start | bytes 1376260
  611.5 182.8 %all-to-all-start.1 = ((bf16[64,2,7168]{2,1,0:T(2,128)(2,1)}), bf16[64,2,7168]{2,1,0:T(2,128)(2,1)}, u32[]{:S(2)}, u32[]{:S(2)}) async-start(bf16[64,2,7168]{2,1,0:T(2,128)(2,1)} %reshape.96), calls=%async_computation.1 | async-start | bytes 3670016 | tf_op jit(solution)/shard_map/all_to_all | solution.py:95
  625.6 3.1 collective-permute-start
  628.7 6.0 collective-permute-start.1
  634.7 162.7 %collective-permute-start.2 = (f32[7168]{0:T(1024)S(1)}, f32[7168]{0:T(1024)S(1)}, u32[]{:S(2)}, u32[]{:S(2)}) collective-permute-start(f32[7168]{0:T(1024)S(1)} %collective-permute-done.1), channel_id=1, source_target_pairs={{0,256},{64,320},{128,384},{192,448},{256,0},{320,64},{384,128},{4... | collective-permute-start | bytes 86024 | tf_op jit(solution)/shard_map/ppermute | solution.py:15
  797.4 7.3 collective-permute-start.3
where the time goes:
time: 806 us; the launch traced here: 805 us
  waiting for transfers between devices  667 us (83%)
  starting transfers between devices  80.1 us (10%)
  local copies, waits for them, and re-layouts  25 us (3%)
  matrix products  22.9 us (3%)
  other arithmetic  9.96 us (1%)
    all_to_all x2, waiting for transfers between devices, per_device(): lax.all_to_all(outgoing, 'ep', split_axis=0, concat_axis=0, tiled=True)  336 us
    all_to_all x2, waiting for transfers between devices, per_device(): lax.all_to_all(partial_value.reshape(received.shape), 'ep', split_axis=0,...  313 us
    all_to_all x2, starting transfers between devices, per_device(): lax.all_to_all(outgoing, 'ep', split_axis=0, concat_axis=0, tiled=True)  39.3 us
    all_to_all x2, starting transfers between devices, per_device(): lax.all_to_all(partial_value.reshape(received.shape), 'ep', split_axis=0,...  19.7 us
  transfers between devices with their start and end apart: 9, of which 8 were waited for; matrix products, arithmetic and copies ran while one was open for 6% of the time, Pallas kernels for 0%

commit v1 on v0

v1 whole, which is shorter than its diff:
```python
import functools

import jax
import jax.numpy as jnp
from jax import lax
from jax.experimental import pallas as pl
from jax.experimental.pallas import tpu as pltpu
from jax.sharding import PartitionSpec as P

CAP = 2
EPSILON = 1e-06
QUARTERS = 4
EXTRA = 128
MESH = pl.DeviceIdType.MESH
F32 = jnp.float32
BF16 = jnp.bfloat16


def route_tables(id_rows, gate_rows, experts):
    tokens = id_rows.shape[0]
    window = id_rows < experts
    labels = jnp.arange(experts, dtype=jnp.int32)
    hit_table = jnp.any(id_rows[:, :, None] == labels[None, None, :], axis=1).astype(F32)
    earlier = (jnp.arange(tokens)[:, None] > jnp.arange(tokens)[None, :]).astype(F32)
    slot_rank = jnp.dot(earlier, hit_table, precision=lax.Precision.HIGHEST)
    slot_ids = jnp.arange(CAP, dtype=F32)
    select = hit_table.T[:, None, :] * (slot_rank.T[:, None, :] == slot_ids[None, :, None]).astype(F32)
    pick_gate = jnp.sum(jnp.where(window, gate_rows, 0.0), axis=1)
    return (select, pick_gate, window)


def row_norm_values(x_rows):
    x_float = x_rows.astype(F32)
    inverse_root_scale = lax.rsqrt(jnp.mean(x_float * x_float, axis=-1, keepdims=True) + EPSILON)
    return (x_float * inverse_root_scale, inverse_root_scale)


def pack_rows(select, values):
    packed = jnp.einsum("ejt,td->ejd", select.astype(BF16), values, preferred_element_type=F32).astype(BF16)
    experts, slots, width = packed.shape
    folded = packed.reshape(2, 2, slots, QUARTERS, width // QUARTERS)
    return folded.transpose(0, 1, 3, 2, 4).reshape(2, 2 * QUARTERS * slots, width // QUARTERS)


def unpack_rows(folded, width):
    parts = folded.reshape(2, 2, QUARTERS, CAP, width // QUARTERS)
    return parts.transpose(0, 1, 3, 2, 4).reshape(4, CAP, width)


def to_tokens(select, per_slot):
    return jnp.einsum("ejt,ejd->td", select, per_slot.astype(F32), precision=lax.Precision.HIGHEST)


def exact_pick(chooser, rows):
    return jnp.dot(chooser, rows, preferred_element_type=F32).astype(BF16)


def ring_kernel(
    ring,
    packed_bwd,
    packed_fwd,
    saved,
    w_gate,
    w_up,
    w_down,
    out_bwd,
    out_fwd,
    gathered,
    came_x,
    acc,
    lhs,
    part_bwd,
    part_fwd,
    sums_bwd,
    sums_fwd,
    back_bwd,
    back_fwd,
    fin_bwd,
    fin_fwd,
    x_send,
    x_recv,
    g_send,
    g_recv,
    r_send,
    r_recv,
):
    half = ring // 2
    reach = half // 2
    span = half - 1 + reach
    pp = lax.axis_index("pp")
    ep = lax.axis_index("ep")
    a = ep // ring
    z = lax.rem(ep, ring)
    h = z // half
    i = lax.rem(z, half)
    quarter = packed_fwd.shape[2]
    hid = w_gate.shape[1]
    packed = (packed_bwd, packed_fwd)
    sums = (sums_bwd, sums_fwd)
    parts = (part_bwd, part_fwd)
    own_left, out_left = ring + half, ring + half + 1

    def at(position, pair=a):
        return (pp, pair * ring + lax.rem(position + 2 * ring, ring))

    partner = at(z, 1 - a)
    ways = ((1, i), (-1, half - 1 - i))

    barrier = pltpu.get_barrier_semaphore()
    for device in (at(z + 1), at(z - 1), partner):
        pl.semaphore_signal(barrier, inc=1, device_id=device, device_id_type=MESH)
    pl.semaphore_wait(barrier, 3)

    def x_copy(b):
        return pltpu.make_async_remote_copy(
            src_ref=packed[b].at[1 - a],
            dst_ref=came_x.at[b],
            send_sem=x_send.at[b],
            recv_sem=x_recv.at[b],
            device_id=partner,
            device_id_type=MESH,
        )

    for b in range(2):
        x_copy(b).start()

    def g_copy(b, source, target, sem, way):
        return pltpu.make_async_remote_copy(
            src_ref=gathered.at[b, source],
            dst_ref=gathered.at[b, target],
            send_sem=g_send.at[b, sem],
            recv_sem=g_recv.at[b, target],
            device_id=at(z + way),
            device_id_type=MESH,
        )

    def g_arrived(b, slot):
        g_copy(b, slot, slot, slot, 1).wait_recv()

    row = lax.broadcasted_iota(jnp.int32, (16, 32), 0)
    col = lax.broadcasted_iota(jnp.int32, (16, 32), 1)

    def merge(portion):
        pair = (row >> 1) & 1
        place = portion * 8 + (row >> 2) * 2 + (row & 1)
        return (col == jnp.where(pair == a, place, place + 16)).astype(BF16)

    def own_sends(b, act):
        for way, depth in ways:
            sem_in = z if way == 1 else own_left
            sem_out = ring + i if way == 1 else out_left

            @pl.when(depth < half - 1)
            def _():
                act(g_copy(b, z, z, sem_in, way))

            @pl.when(depth >= reach)
            def _():
                act(g_copy(b, ring + i, jnp.where(depth < half - 1, ring + i, z), sem_out, way))

    def begin(b):
        x_copy(b).wait_recv()
        rows = jnp.concatenate([packed[b][a], came_x[b]], axis=0)
        gathered[b, z] = exact_pick(merge(h), rows)
        gathered[b, ring + i] = exact_pick(merge(1 - h), rows)
        own_sends(b, lambda c: c.start())

    def gather_step(b, t, arrived, act):
        for way, depth in ways:
            source = lax.rem(z - way * t + ring, ring)

            @pl.when(t <= depth + reach)
            def _():
                if arrived:
                    g_arrived(b, source)

                @pl.when(depth < half - 1)
                def _():
                    act(g_copy(b, source, source, source, way))

            @pl.when(t <= depth - reach)
            def _():
                slot = ring + i - way * t
                if arrived:
                    g_arrived(b, slot)
                act(g_copy(b, slot, jnp.where(depth < half - 1, slot, source), slot, way))

    def r_copy(b, source, target, way):
        return pltpu.make_async_remote_copy(
            src_ref=sums[b].at[source],
            dst_ref=sums[b].at[target],
            send_sem=r_send.at[b, source],
            recv_sem=r_recv.at[b, target],
            device_id=at(z - way),
            device_id_type=MESH,
        )

    def r_arrived(b, slot):
        r_copy(b, slot, slot, 1).wait_recv()

    def rounded(b, total):
        if b == 1:
            return total.astype(BF16)
        score = total[0:8, quarter:] + total[8:16, quarter:]
        high = score.astype(BF16).astype(F32)
        tail = jnp.concatenate([high, score - high], axis=0)
        return jnp.concatenate([total[:, :quarter], tail], axis=1).astype(BF16)

    def reduce_target(way, depth, t, dest):
        local = jnp.where(t == 1, own_left, dest) if way == -1 else dest
        return jnp.where(depth > 0, local, ring + lax.rem(dest, half))

    def reduce_step(b, t):
        for way, depth in ways:
            dest = lax.rem(z - way * t + ring, ring)

            @pl.when(t <= depth + reach)
            def _():
                @pl.when(depth < half - 1)
                def _():
                    r_arrived(b, dest)
                    sums[b][dest] = rounded(b, sums[b][dest].astype(F32) + parts[b][dest])

                @pl.when(depth == half - 1)
                def _():
                    sums[b][dest] = rounded(b, parts[b][dest])

                r_copy(b, dest, reduce_target(way, depth, t, dest), way).start()

            @pl.when(t <= depth - reach)
            def _():
                slot = ring + i - way * t
                r_arrived(b, slot)
                r_copy(b, slot, slot, way).start()

    def reduce_drain(b, t):
        for way, depth in ways:
            dest = lax.rem(z - way * t + ring, ring)

            @pl.when(t <= depth + reach)
            def _():
                r_copy(b, dest, dest, way).wait_send()

            @pl.when(t <= depth - reach)
            def _():
                slot = ring + i - way * t
                r_copy(b, slot, slot, way).wait_send()

    rows_all = ring * 16
    row_quarter = (lax.broadcasted_iota(jnp.int32, (rows_all, 1), 0) >> 2) & 3

    def folded(value):
        width = value.shape[1]
        pairs = value.reshape(ring, 2, 8, width)
        total = pairs[:, 0] + pairs[:, 1]
        total = total + pltpu.roll(total, 4, 1)
        return total.reshape(ring * 8, width)

    def spread(value):
        width = value.shape[1]
        tiles = value.reshape(ring, 1, 8, width)
        return jnp.concatenate([tiles, tiles], axis=1).reshape(rows_all, width)

    def block(q):
        return slice(q * quarter, (q + 1) * quarter)

    nt = (((1,), (1,)), ((), ()))

    def compute_bwd():
        rows = gathered[0, 0:ring].reshape(rows_all, quarter)
        for q in range(QUARTERS):
            piece = lax.dot_general(rows, w_down[:, block(q)], nt, preferred_element_type=F32)
            acc[:, :hid] = piece if q == 0 else jnp.where(row_quarter == q, piece, acc[:, :hid])
        grad_act = folded(acc[:, :hid])
        pre_gate = saved[0]
        pre_up = saved[1]
        sig = jax.nn.sigmoid(pre_gate)
        silu = pre_gate * sig
        active = (silu * pre_up).astype(BF16).astype(F32)
        grad_gate = grad_act * pre_up * sig * (1.0 + pre_gate * (1.0 - sig))
        grad_up = grad_act * silu
        score = jnp.sum(grad_act * active, axis=1, keepdims=True)
        score = jnp.broadcast_to(score, (ring * 8, EXTRA)).reshape(ring, 8, EXTRA)
        both = spread(jnp.concatenate([grad_gate, grad_up], axis=1))
        for q in range(QUARTERS):
            lhs[:, 2 * hid * q : 2 * hid * (q + 1)] = jnp.where(row_quarter == q, both, 0.0).astype(BF16)
        part_bwd[:, 0:8, quarter:] = score
        part_bwd[:, 8:16, quarter:] = jnp.zeros_like(score)
        total = None
        for q in range(QUARTERS):
            weights = jnp.concatenate([w_gate[block(q), :], w_up[block(q), :]], axis=1)
            piece = lax.dot_general(
                lhs[:, 2 * hid * q : 2 * hid * (q + 1)], weights, nt, preferred_element_type=F32
            ).reshape(ring, 16, quarter)
            if q == 0:
                part_bwd[:, :, :quarter] = piece
            else:
                part_bwd[:, :, :quarter] += piece

    def compute_fwd():
        rows = gathered[1, 0:ring].reshape(rows_all, quarter)
        for q in range(QUARTERS):
            weights = jnp.concatenate([w_gate[block(q), :], w_up[block(q), :]], axis=1)
            piece = jnp.dot(rows, weights, preferred_element_type=F32)
            acc[...] = piece if q == 0 else jnp.where(row_quarter == q, piece, acc[...])
        z_both = folded(acc[...])
        z_gate = z_both[:, :hid]
        active = spread(z_gate * jax.nn.sigmoid(z_gate) * z_both[:, hid:])
        for q in range(QUARTERS):
            lhs[:, hid * q : hid * (q + 1)] = jnp.where(row_quarter == q, active, 0.0).astype(BF16)
        weights = jnp.concatenate([w_down[:, block(q)] for q in range(QUARTERS)], axis=0)
        part_fwd[...] = jnp.dot(
            lhs[:, : hid * QUARTERS], weights, preferred_element_type=F32
        ).reshape(ring, 16, quarter)

    for b in range(2):
        begin(b)

    @pl.loop(1, span + 1)
    def _(t):
        gather_step(0, t, True, lambda c: c.start())
        gather_step(1, t, True, lambda c: c.start())

    compute_bwd()
    compute_fwd()

    @pl.loop(0, span)
    def _(k):
        reduce_step(0, span - k)
        reduce_step(1, span - k)

    backs = (back_bwd, back_fwd)
    fins = (fin_bwd, fin_fwd)
    outs = (out_bwd, out_fwd)

    def b_copy(b):
        return pltpu.make_async_remote_copy(
            src_ref=fins[b],
            dst_ref=backs[b],
            send_sem=x_send.at[2 + b],
            recv_sem=x_recv.at[2 + b],
            device_id=partner,
            device_id_type=MESH,
        )

    def compact(pair):
        place = (row & 1) + ((row >> 1) & 3) * 4 + pair * 2
        return (col == jnp.where((row >> 3) == h, place, place + 16)).astype(BF16)

    def finish(b):
        @pl.when(i < half - 1)
        def _():
            r_arrived(b, z)
            parts[b][z] += sums[b][z].astype(F32)

        @pl.when(i > 0)
        def _():
            r_arrived(b, own_left)
            parts[b][z] += sums[b][own_left].astype(F32)

        r_arrived(b, ring + i)
        rows = jnp.concatenate([rounded(b, parts[b][z]), sums[b][ring + i]], axis=0)
        fins[b][...] = exact_pick(compact(1 - a), rows)
        b_copy(b).start()
        outs[b][a] = exact_pick(compact(a), rows)

    finish(0)
    finish(1)
    for b in range(2):
        b_copy(b).wait_recv()
        outs[b][1 - a] = backs[b][...]
        b_copy(b).wait_send()
        x_copy(b).wait_send()
        own_sends(b, lambda c: c.wait_send())

    @pl.loop(1, span + 1)
    def _(t):
        for b in range(2):
            gather_step(b, t, False, lambda c: c.wait_send())
            reduce_drain(b, t)


def exchange(packed_bwd, packed_fwd, saved, w_gate, w_up, w_down, ring):
    quarter = packed_fwd.shape[2]
    hid = w_gate.shape[1]
    wide = quarter + EXTRA
    half = ring // 2
    slots = ring + half + 2
    rows_all = ring * 16
    vmem = pl.BlockSpec(memory_space=pltpu.VMEM)
    return pl.pallas_call(
        functools.partial(ring_kernel, ring),
        out_shape=(
            jax.ShapeDtypeStruct((2, 16, wide), BF16),
            jax.ShapeDtypeStruct((2, 16, quarter), BF16),
        ),
        in_specs=[vmem] * 6,
        out_specs=(vmem, vmem),
        scratch_shapes=[
            pltpu.VMEM((2, ring + half, 16, quarter), BF16),
            pltpu.VMEM((2, 16, quarter), BF16),
            pltpu.VMEM((rows_all, 2 * hid), F32),
            pltpu.VMEM((rows_all, 2 * hid * QUARTERS), BF16),
            pltpu.VMEM((ring, 16, wide), F32),
            pltpu.VMEM((ring, 16, quarter), F32),
            pltpu.VMEM((slots, 16, wide), BF16),
            pltpu.VMEM((slots, 16, quarter), BF16),
            pltpu.VMEM((16, wide), BF16),
            pltpu.VMEM((16, quarter), BF16),
            pltpu.VMEM((16, wide), BF16),
            pltpu.VMEM((16, quarter), BF16),
            pltpu.SemaphoreType.DMA((4,)),
            pltpu.SemaphoreType.DMA((4,)),
            pltpu.SemaphoreType.DMA((2, slots)),
            pltpu.SemaphoreType.DMA((2, slots)),
            pltpu.SemaphoreType.DMA((2, slots)),
            pltpu.SemaphoreType.DMA((2, slots)),
        ],
        compiler_params=pltpu.CompilerParams(
            collective_id=0, has_side_effects=True, vmem_limit_bytes=52 * 1024 * 1024
        ),
        cost_estimate=pl.CostEstimate(
            flops=24 * ring * 4 * quarter * 4 * hid, bytes_accessed=24 * quarter * hid, transcendentals=0
        ),
    )(packed_bwd, packed_fwd, saved, w_gate, w_up, w_down)


def per_device(
    forward_input_rows,
    ids_fwd,
    gate_fwd,
    backward_input_rows,
    dy_bwd,
    ids_bwd,
    gate_bwd,
    saved_z,
    norm_gain,
    w_gate,
    w_up,
    w_down,
):
    experts = 4
    ring = lax.axis_size("ep") // 2
    gain_vector_row = norm_gain[0]
    width = forward_input_rows.shape[2]
    hid = w_gate.shape[1]
    select_b, pick_gate_b, window = route_tables(ids_bwd[0], gate_bwd[0], experts)
    packed_bwd = pack_rows(select_b, dy_bwd[0])
    select_f, pick_gate_f, _ = route_tables(ids_fwd[0], gate_fwd[0], experts)
    xhat, _ = row_norm_values(forward_input_rows[0])
    packed_fwd = pack_rows(select_f, (xhat * gain_vector_row).astype(BF16))
    saved = saved_z[0].reshape(2, 2, ring, CAP, hid).transpose(0, 2, 1, 3, 4)
    saved = jnp.broadcast_to(saved.reshape(2, ring, 1, 2 * CAP, hid), (2, ring, 2, 2 * CAP, hid))
    saved = saved.reshape(2, ring * 8, hid).astype(F32)
    back, forward = exchange(packed_bwd, packed_fwd, saved, w_gate, w_up, w_down, ring)
    quarter = width // QUARTERS
    per_slot = unpack_rows(forward, width)
    y_rows = (pick_gate_f[:, None] * to_tokens(select_f, per_slot)).astype(BF16)[None]
    score = back[:, :, quarter].reshape(2, 2, QUARTERS, CAP).astype(F32)
    score = (score[:, :, 0] + score[:, :, 2]).reshape(experts, CAP)
    token_score = jnp.einsum("ejt,ej->t", select_b, score, precision=lax.Precision.HIGHEST)
    grad_picks = jnp.where(window, token_score[:, None], 0.0)[None]
    per_slot = unpack_rows(back[:, :, :quarter], width)
    grad_normed = pick_gate_b[:, None] * to_tokens(select_b, per_slot)
    xhat, inverse = row_norm_values(backward_input_rows[0])
    gain_term = jnp.sum(grad_normed * xhat, axis=0)
    count = lax.axis_size("pp")
    mirrored = lax.ppermute(gain_term, "pp", [(p, count - 1 - p) for p in range(count)])
    scaled = grad_normed * gain_vector_row
    grad_rows = inverse * (scaled - xhat * jnp.mean(scaled * xhat, axis=-1, keepdims=True))
    return (y_rows, grad_rows.astype(BF16)[None], grad_picks, (gain_term + mirrored)[None, None])


def solution(mesh):
    rows = P("pp", "ep", None)
    return jax.shard_map(
        per_device,
        mesh=mesh,
        in_specs=(
            rows,
            rows,
            rows,
            rows,
            rows,
            rows,
            rows,
            P("pp", None, "ep", None),
            P("pp", None),
            P(None, "ep"),
            P(None, "ep"),
            P("ep", None),
        ),
        out_specs=(rows, rows, rows, rows),
        check_vma=False,
    )
```

time: 806 us -> 234 us (0.29)
  the two profiles are of different devices: /device:TPU:96 before, /device:TPU:1 now
where the time goes in v1:
time: 234 us; the launch traced here: 233 us
  Pallas kernels  184 us (79%)
  starting transfers between devices  37.5 us (16%)
  other arithmetic  5.34 us (2%)
  matrix products  4.28 us (2%)
    pallas_call x1, Pallas kernels, exchange(): pl.pallas_call(functools.partial(ring_kernel, ring), out_shape=(jax.Shape...  184 us
    ppermute x1, starting transfers between devices, per_device(): lax.ppermute(gain_term, 'pp', [(p, count - 1 - p) for p in range(count)])  37.5 us
  transfers between devices with their start and end apart: 1, of which 0 were waited for; matrix products, arithmetic and copies ran while one was open for 2% of the time, Pallas kernels for 0%

profile of v1, /device:TPU:1, one launch (start us, length us, event | category | flops | bytes accessed | tf_op | source)
XLA Modules:
  0.0 233.5 jit_solution(4086111586038822139)
XLA Ops:
  0.6 0.0 copy-start
  0.6 0.0 copy-start.2
  0.7 0.8 fusion.25
  1.4 0.1 fusion.24
  1.6 0.7 fusion.26
  2.3 0.1 fusion.23
  2.4 1.2 fusion.7
  3.6 1.3 convolution_convert_fusion
  5.0 0.1 copy.53
  5.2 0.0 copy-done
  5.2 0.2 convolution_convert_fusion.1
  5.4 0.1 copy.54
  5.6 0.0 copy-done.2
  5.6 0.1 copy.43
  5.7 0.0 copy-start.1
  5.8 0.0 copy-start.3
  5.8 0.0 copy-start.6
  5.8 0.0 copy-start.4
  5.8 184.4 %shard_map.147 = (bf16[2,16,1920]{2,1,0:T(8,128)(2,1)S(1)}, bf16[2,16,1792]{2,1,0:T(8,128)(2,1)S(1)}) custom-call(bf16[2,16,1792]{2,1,0:T(8,128)(2,1)S(1)} %reshape.85.packed_bwd, bf16[2,16,1792]{2,1,0:T(8,128)(2,1)S(1)} %reshape.87.packed_fwd, f32[2,256,128]{2,1,0:T(8,128)S(1)} %bitcast.88, bf16[7168,128]{1,0:T(8,128)(2,1)} %w_gate.1, ...), custom_call_target="tpu_custom_call" | custom-call | flops 2818572288 | bytes 5505024 | tf_op jit(solution)/shard_map/pallas_call | solution.py:391
  190.4 0.0 copy-start.5
  190.4 0.0 copy-start.7
  190.4 0.0 copy-done.1
  190.4 0.2 fusion.15
  190.7 0.0 copy-done.3
  190.7 0.0 copy-done.6
  190.7 0.0 copy-done.4
  190.7 1.0 fusion.14
  191.7 37.5 %collective-permute-start = (f32[7168]{0:T(1024)S(1)}, f32[7168]{0:T(1024)S(1)}, u32[]{:S(2)}, u32[]{:S(2)}) collective-permute-start(f32[7168]{0:T(1024)S(1)} %get-tuple-element.8), channel_id=1, source_target_pairs={{0,960},{64,896},{128,832},{192,768},{256,704},{320,640},{384,576}... | collective-permute-start | bytes 86024 | tf_op jit(solution)/shard_map/ppermute | solution.py:468
  229.2 0.1 convert_reduce_fusion
  229.3 0.1 reshape.95
  229.4 0.1 copy.47
  229.5 0.2 convolution_bitcast_fusion.2
  229.7 0.6 compare_select_fusion
  230.4 0.0 copy-done.5
  230.5 0.0 copy-done.7
  230.5 1.0 fusion.16
  231.5 1.4 fusion.3
  232.9 0.0 collective-permute-done
  232.9 0.6 add.30
  (22 shorter events, 0.6 us)
Async XLA Ops:
  0.6 4.5 %copy-start = (bf16[1,32,7168]{2,1,0:T(8,128)(2,1)S(1)}, bf16[1,32,7168]{2,1,0:T(8,128)(2,1)}, u32[]{:S(2)}) copy-start(bf16[1,32,7168]{2,1,0:T(8,128)(2,1)} %param.16) | copy-start | bytes 1376260
  0.6 4.9 %copy-start.2 = (bf16[1,2,128,128]{3,2,1,0:T(8,128)(2,1)S(1)}, bf16[1,2,128,128]{3,2,1,0:T(8,128)(2,1)}, u32[]{:S(2)}) copy-start(bf16[1,2,128,128]{3,2,1,0:T(8,128)(2,1)} %param.19) | copy-start | bytes 196612
  5.7 184.7 %copy-start.1 = (bf16[1,32,7168]{2,1,0:T(8,128)(2,1)S(1)}, bf16[1,32,7168]{2,1,0:T(8,128)(2,1)}, u32[]{:S(2)}) copy-start(bf16[1,32,7168]{2,1,0:T(8,128)(2,1)} %param.15) | copy-start | bytes 1376260
  5.8 184.9 %copy-start.3 = (s32[1,32,8]{1,2,0:T(8,128)S(1)}, s32[1,32,8]{1,2,0:T(8,128)}, u32[]{:S(2)}) copy-start(s32[1,32,8]{1,2,0:T(8,128)} %param.17) | copy-start | bytes 3076
  5.8 184.9 %copy-start.6 = (f32[1,32,8]{1,2,0:T(8,128)S(1)}, f32[1,32,8]{1,2,0:T(8,128)}, u32[]{:S(2)}) copy-start(f32[1,32,8]{1,2,0:T(8,128)} %param.18) | copy-start | bytes 3076
  5.8 184.9 %copy-start.4 = (f32[1,7168]{1,0:T(1,128)S(1)}, f32[1,7168]{1,0:T(1,128)}, u32[]{:S(2)}) copy-start(f32[1,7168]{1,0:T(1,128)} %param.20) | copy-start | bytes 86020
  190.4 40.1 %copy-start.5 = (s32[1,32,8]{1,2,0:T(8,128)S(1)}, s32[1,32,8]{1,2,0:T(8,128)}, u32[]{:S(2)}) copy-start(s32[1,32,8]{1,2,0:T(8,128)} %param.13) | copy-start | bytes 3076
  190.4 40.1 %copy-start.7 = (f32[1,32,8]{1,2,0:T(8,128)S(1)}, f32[1,32,8]{1,2,0:T(8,128)}, u32[]{:S(2)}) copy-start(f32[1,32,8]{1,2,0:T(8,128)} %param.14) | copy-start | bytes 3076
  191.7 41.2 %collective-permute-start = (f32[7168]{0:T(1024)S(1)}, f32[7168]{0:T(1024)S(1)}, u32[]{:S(2)}, u32[]{:S(2)}) collective-permute-start(f32[7168]{0:T(1024)S(1)} %get-tuple-element.8), channel_id=1, source_target_pairs={{0,960},{64,896},{128,832},{192,768},{256,704},{320,640},{384,576}... | collective-permute-start | bytes 86024 | tf_op jit(solution)/shard_map/ppermute | solution.py:468

commit v2 on v1

--- a/solution.py
+++ b/solution.py
@@ -85,8 +85,6 @@
     r_recv,
 ):
     half = ring // 2
-    reach = half // 2
-    span = half - 1 + reach
     pp = lax.axis_index("pp")
     ep = lax.axis_index("ep")
     a = ep // ring
@@ -104,7 +102,7 @@
         return (pp, pair * ring + lax.rem(position + 2 * ring, ring))
 
     partner = at(z, 1 - a)
-    ways = ((1, i), (-1, half - 1 - i))
+    ways = ((1, i, half), (-1, half - 1 - i, half - 1))
 
     barrier = pltpu.get_barrier_semaphore()
     for device in (at(z + 1), at(z - 1), partner):
@@ -146,7 +144,7 @@
         return (col == jnp.where(pair == a, place, place + 16)).astype(BF16)
 
     def own_sends(b, act):
-        for way, depth in ways:
+        for way, depth, reach in ways:
             sem_in = z if way == 1 else own_left
             sem_out = ring + i if way == 1 else out_left
 
@@ -154,7 +152,7 @@
             def _():
                 act(g_copy(b, z, z, sem_in, way))
 
-            @pl.when(depth >= reach)
+            @pl.when(depth >= half - reach)
             def _():
                 act(g_copy(b, ring + i, jnp.where(depth < half - 1, ring + i, z), sem_out, way))
 
@@ -166,24 +164,34 @@
         own_sends(b, lambda c: c.start())
 
     def gather_step(b, t, arrived, act):
-        for way, depth in ways:
+        for way, depth, reach in ways:
             source = lax.rem(z - way * t + ring, ring)
 
-            @pl.when(t <= depth + reach)
+            @pl.when((t < reach) & (depth < half - 1))
             def _():
                 if arrived:
                     g_arrived(b, source)
-
-                @pl.when(depth < half - 1)
-                def _():
-                    act(g_copy(b, source, source, source, way))
-
-            @pl.when(t <= depth - reach)
+                act(g_copy(b, source, source, source, way))
+
+            @pl.when(t <= depth - half + reach)
             def _():
                 slot = ring + i - way * t
                 if arrived:
                     g_arrived(b, slot)
                 act(g_copy(b, slot, jnp.where(depth < half - 1, slot, source), slot, way))
+
+    def gather_rest(b):
+        for way, depth, reach in ways:
+
+            @pl.when(depth < half - 1)
+            def _():
+                g_arrived(b, lax.rem(z - way * reach + ring, ring))
+
+            @pl.when(depth == half - 1)
+            def _():
+                @pl.loop(1, reach + 1)
+                def _(t):
+                    g_arrived(b, lax.rem(z - way * t + ring, ring))
 
     def r_copy(b, source, target, way):
         return pltpu.make_async_remote_copy(
@@ -206,42 +214,44 @@
         tail = jnp.concatenate([high, score - high], axis=0)
         return jnp.concatenate([total[:, :quarter], tail], axis=1).astype(BF16)
 
-    def reduce_target(way, depth, t, dest):
-        local = jnp.where(t == 1, own_left, dest) if way == -1 else dest
-        return jnp.where(depth > 0, local, ring + lax.rem(dest, half))
-
     def reduce_step(b, t):
-        for way, depth in ways:
+        for way, depth, reach in ways:
             dest = lax.rem(z - way * t + ring, ring)
-
-            @pl.when(t <= depth + reach)
-            def _():
-                @pl.when(depth < half - 1)
+            local, other = dest, ring + lax.rem(dest, half)
+            if way == -1:
+                local = jnp.where(t == 1, own_left, local)
+                other = jnp.where(t == 1, out_left, other)
+
+            @pl.when(t <= reach)
+            def _():
+                chained = (t < reach) & (depth < half - 1)
+
+                @pl.when(chained)
                 def _():
                     r_arrived(b, dest)
                     sums[b][dest] = rounded(b, sums[b][dest].astype(F32) + parts[b][dest])
 
-                @pl.when(depth == half - 1)
+                @pl.when(jnp.logical_not(chained))
                 def _():
                     sums[b][dest] = rounded(b, parts[b][dest])
 
-                r_copy(b, dest, reduce_target(way, depth, t, dest), way).start()
-
-            @pl.when(t <= depth - reach)
+                r_copy(b, dest, jnp.where(depth > 0, local, other), way).start()
+
+            @pl.when(t <= depth - half + reach)
             def _():
                 slot = ring + i - way * t
                 r_arrived(b, slot)
-                r_copy(b, slot, slot, way).start()
+                r_copy(b, slot, other, way).start()
 
     def reduce_drain(b, t):
-        for way, depth in ways:
+        for way, depth, reach in ways:
             dest = lax.rem(z - way * t + ring, ring)
 
-            @pl.when(t <= depth + reach)
+            @pl.when(t <= reach)
             def _():
                 r_copy(b, dest, dest, way).wait_send()
 
-            @pl.when(t <= depth - reach)
+            @pl.when(t <= depth - half + reach)
             def _():
                 slot = ring + i - way * t
                 r_copy(b, slot, slot, way).wait_send()
@@ -286,7 +296,6 @@
             lhs[:, 2 * hid * q : 2 * hid * (q + 1)] = jnp.where(row_quarter == q, both, 0.0).astype(BF16)
         part_bwd[:, 0:8, quarter:] = score
         part_bwd[:, 8:16, quarter:] = jnp.zeros_like(score)
-        total = None
         for q in range(QUARTERS):
             weights = jnp.concatenate([w_gate[block(q), :], w_up[block(q), :]], axis=1)
             piece = lax.dot_general(
@@ -313,21 +322,32 @@
             lhs[:, : hid * QUARTERS], weights, preferred_element_type=F32
         ).reshape(ring, 16, quarter)
 
-    for b in range(2):
-        begin(b)
-
-    @pl.loop(1, span + 1)
+    begin(0)
+    begin(1)
+
+    def send(copy):
+        copy.start()
+
+    gather_step(0, 1, True, send)
+
+    @pl.loop(1, half)
     def _(t):
-        gather_step(0, t, True, lambda c: c.start())
-        gather_step(1, t, True, lambda c: c.start())
-
+        gather_step(1, t, True, send)
+        gather_step(0, t + 1, True, send)
+
+    gather_rest(0)
     compute_bwd()
+    gather_step(1, half, True, send)
+    reduce_step(0, half)
+    gather_rest(1)
     compute_fwd()
 
-    @pl.loop(0, span)
+    @pl.loop(0, half - 1)
     def _(k):
-        reduce_step(0, span - k)
-        reduce_step(1, span - k)
+        reduce_step(1, half - k)
+        reduce_step(0, half - 1 - k)
+
+    reduce_step(1, 1)
 
     backs = (back_bwd, back_fwd)
     fins = (fin_bwd, fin_fwd)
@@ -359,6 +379,13 @@
             parts[b][z] += sums[b][own_left].astype(F32)
 
         r_arrived(b, ring + i)
+
+        @pl.when(i < half - 1)
+        def _():
+            r_arrived(b, out_left)
+            added = sums[b][ring + i].astype(F32) + sums[b][out_left].astype(F32)
+            sums[b][ring + i] = rounded(b, added)
+
         rows = jnp.concatenate([rounded(b, parts[b][z]), sums[b][ring + i]], axis=0)
         fins[b][...] = exact_pick(compact(1 - a), rows)
         b_copy(b).start()
@@ -373,7 +400,7 @@
         x_copy(b).wait_send()
         own_sends(b, lambda c: c.wait_send())
 
-    @pl.loop(1, span + 1)
+    @pl.loop(1, half + 1)
     def _(t):
         for b in range(2):
             gather_step(b, t, False, lambda c: c.wait_send())

time: 234 us -> 213 us (0.910)
  starting transfers between devices: 37.5 us -> 13 us
  Pallas kernels: 184 us -> 189 us
    ppermute x1, starting transfers between devices: 37.5 us -> 13 us  [per_device(): lax.ppermute(gain_term, 'pp', [(p, count - 1 - p) for p in range(count)])]
    pallas_call x1, Pallas kernels: 184 us -> 189 us  [exchange(): pl.pallas_call(functools.partial(ring_kernel, ring), out_shape=(jax.Shape...]
where the time goes in v2:
time: 213 us
  Pallas kernels  189 us (89%)
  starting transfers between devices  13 us (6%)
  other arithmetic  5.34 us (3%)
  matrix products  4.28 us (2%)
    pallas_call x1, Pallas kernels, exchange(): pl.pallas_call(functools.partial(ring_kernel, ring), out_shape=(jax.Shape...  189 us
    ppermute x1, starting transfers between devices, per_device(): lax.ppermute(gain_term, 'pp', [(p, count - 1 - p) for p in range(count)])  13 us
  transfers between devices with their start and end apart: 1, of which 0 were waited for; matrix products, arithmetic and copies ran while one was open for 2% of the time, Pallas kernels for 0%

profile of v2, /device:TPU:1, one launch (start us, length us, event | category | flops | bytes accessed | tf_op | source)
XLA Modules:
  0.0 213.2 jit_solution(8498648698409133538)
XLA Ops:
  0.6 0.0 copy-start
  0.6 0.0 copy-start.2
  0.7 0.8 fusion.25
  1.4 0.1 fusion.24
  1.6 0.7 fusion.26
  2.3 0.1 fusion.23
  2.4 1.2 fusion.7
  3.6 1.3 convolution_convert_fusion
  5.0 0.1 copy.53
  5.2 0.0 copy-done
  5.2 0.2 convolution_convert_fusion.1
  5.4 0.1 copy.54
  5.6 0.0 copy-done.2
  5.6 0.1 copy.43
  5.7 0.0 copy-start.1
  5.8 0.0 copy-start.3
  5.8 0.0 copy-start.6
  5.8 0.0 copy-start.4
  5.8 188.6 %shard_map.147 = (bf16[2,16,1920]{2,1,0:T(8,128)(2,1)S(1)}, bf16[2,16,1792]{2,1,0:T(8,128)(2,1)S(1)}) custom-call(bf16[2,16,1792]{2,1,0:T(8,128)(2,1)S(1)} %reshape.85.packed_bwd, bf16[2,16,1792]{2,1,0:T(8,128)(2,1)S(1)} %reshape.87.packed_fwd, f32[2,256,128]{2,1,0:T(8,128)S(1)} %bitcast.88, bf16[7168,128]{1,0:T(8,128)(2,1)} %w_gate.1, ...), custom_call_target="tpu_custom_call" | custom-call | flops 2818572288 | bytes 5505024 | tf_op jit(solution)/shard_map/pallas_call | solution.py:418
  194.5 0.0 copy-start.5
  194.5 0.0 copy-start.7
  194.6 0.0 copy-done.1
  194.6 0.2 fusion.15
  194.8 0.0 copy-done.3
  194.8 0.0 copy-done.6
  194.9 0.0 copy-done.4
  194.9 1.0 fusion.14
  195.8 13.0 %collective-permute-start = (f32[7168]{0:T(1024)S(1)}, f32[7168]{0:T(1024)S(1)}, u32[]{:S(2)}, u32[]{:S(2)}) collective-permute-start(f32[7168]{0:T(1024)S(1)} %get-tuple-element.8), channel_id=1, source_target_pairs={{0,960},{64,896},{128,832},{192,768},{256,704},{320,640},{384,576}... | collective-permute-start | bytes 86024 | tf_op jit(solution)/shard_map/ppermute | solution.py:495
  208.9 0.1 convert_reduce_fusion
  209.0 0.1 reshape.95
  209.0 0.1 copy.47
  209.1 0.2 convolution_bitcast_fusion.2
  209.3 0.6 compare_select_fusion
  210.1 0.0 copy-done.5
  210.1 0.0 copy-done.7
  210.2 1.0 fusion.16
  211.2 1.4 fusion.3
  212.5 0.0 collective-permute-done
  212.5 0.6 add.30
  (22 shorter events, 0.6 us)
Async XLA Ops:
  0.6 4.5 %copy-start = (bf16[1,32,7168]{2,1,0:T(8,128)(2,1)S(1)}, bf16[1,32,7168]{2,1,0:T(8,128)(2,1)}, u32[]{:S(2)}) copy-start(bf16[1,32,7168]{2,1,0:T(8,128)(2,1)} %param.16) | copy-start | bytes 1376260
  0.6 4.9 %copy-start.2 = (bf16[1,2,128,128]{3,2,1,0:T(8,128)(2,1)S(1)}, bf16[1,2,128,128]{3,2,1,0:T(8,128)(2,1)}, u32[]{:S(2)}) copy-start(bf16[1,2,128,128]{3,2,1,0:T(8,128)(2,1)} %param.19) | copy-start | bytes 196612
  5.7 188.8 %copy-start.1 = (bf16[1,32,7168]{2,1,0:T(8,128)(2,1)S(1)}, bf16[1,32,7168]{2,1,0:T(8,128)(2,1)}, u32[]{:S(2)}) copy-start(bf16[1,32,7168]{2,1,0:T(8,128)(2,1)} %param.15) | copy-start | bytes 1376260
  5.8 189.1 %copy-start.3 = (s32[1,32,8]{1,2,0:T(8,128)S(1)}, s32[1,32,8]{1,2,0:T(8,128)}, u32[]{:S(2)}) copy-start(s32[1,32,8]{1,2,0:T(8,128)} %param.17) | copy-start | bytes 3076
  5.8 189.1 %copy-start.6 = (f32[1,32,8]{1,2,0:T(8,128)S(1)}, f32[1,32,8]{1,2,0:T(8,128)}, u32[]{:S(2)}) copy-start(f32[1,32,8]{1,2,0:T(8,128)} %param.18) | copy-start | bytes 3076
  5.8 189.1 %copy-start.4 = (f32[1,7168]{1,0:T(1,128)S(1)}, f32[1,7168]{1,0:T(1,128)}, u32[]{:S(2)}) copy-start(f32[1,7168]{1,0:T(1,128)} %param.20) | copy-start | bytes 86020
  194.5 15.6 %copy-start.5 = (s32[1,32,8]{1,2,0:T(8,128)S(1)}, s32[1,32,8]{1,2,0:T(8,128)}, u32[]{:S(2)}) copy-start(s32[1,32,8]{1,2,0:T(8,128)} %param.13) | copy-start | bytes 3076
  194.5 15.6 %copy-start.7 = (f32[1,32,8]{1,2,0:T(8,128)S(1)}, f32[1,32,8]{1,2,0:T(8,128)}, u32[]{:S(2)}) copy-start(f32[1,32,8]{1,2,0:T(8,128)} %param.14) | copy-start | bytes 3076
  195.8 16.7 %collective-permute-start = (f32[7168]{0:T(1024)S(1)}, f32[7168]{0:T(1024)S(1)}, u32[]{:S(2)}, u32[]{:S(2)}) collective-permute-start(f32[7168]{0:T(1024)S(1)} %get-tuple-element.8), channel_id=1, source_target_pairs={{0,960},{64,896},{128,832},{192,768},{256,704},{320,640},{384,576}... | collective-permute-start | bytes 86024 | tf_op jit(solution)/shard_map/ppermute | solution.py:495

commit v3 on v2

--- a/solution.py
+++ b/solution.py
@@ -42,13 +42,10 @@
     return folded.transpose(0, 1, 3, 2, 4).reshape(2, 2 * QUARTERS * slots, width // QUARTERS)
 
 
-def unpack_rows(folded, width):
-    parts = folded.reshape(2, 2, QUARTERS, CAP, width // QUARTERS)
-    return parts.transpose(0, 1, 3, 2, 4).reshape(4, CAP, width)
-
-
-def to_tokens(select, per_slot):
-    return jnp.einsum("ejt,ejd->td", select, per_slot.astype(F32), precision=lax.Precision.HIGHEST)
+def slot_picks(select):
+    experts, slots, tokens = select.shape
+    picks = jnp.broadcast_to(select[:, None], (experts, QUARTERS, slots, tokens))
+    return picks.reshape(experts * QUARTERS * slots, tokens).T
 
 
 def exact_pick(chooser, rows):
@@ -63,8 +60,21 @@
     w_gate,
     w_up,
     w_down,
+    x_bwd,
+    gain,
+    pick_bwd,
+    pick_fwd,
+    scale_bwd,
+    scale_fwd,
+    y_out,
+    grad_x,
+    score_out,
+    gain_out,
     out_bwd,
     out_fwd,
+    gain_own,
+    gain_came,
+    inverse,
     gathered,
     came_x,
     acc,
@@ -102,12 +112,17 @@
         return (pp, pair * ring + lax.rem(position + 2 * ring, ring))
 
     partner = at(z, 1 - a)
-    ways = ((1, i, half), (-1, half - 1 - i, half - 1))
+    ways = (
+        ((1, i, half), (-1, half - 1 - i, half - 1)),
+        ((1, i, half - 1), (-1, half - 1 - i, half)),
+    )
 
     barrier = pltpu.get_barrier_semaphore()
-    for device in (at(z + 1), at(z - 1), partner):
+    pairs = lax.axis_size("pp")
+    mirror = (pairs - 1 - pp, ep)
+    for device in (at(z + 1), at(z - 1), partner) + ((mirror,) if pairs > 1 else ()):
         pl.semaphore_signal(barrier, inc=1, device_id=device, device_id_type=MESH)
-    pl.semaphore_wait(barrier, 3)
+    pl.semaphore_wait(barrier, 4 if pairs > 1 else 3)
 
     def x_copy(b):
         return pltpu.make_async_remote_copy(
@@ -144,7 +159,7 @@
         return (col == jnp.where(pair == a, place, place + 16)).astype(BF16)
 
     def own_sends(b, act):
-        for way, depth, reach in ways:
+        for way, depth, reach in ways[b]:
             sem_in = z if way == 1 else own_left
             sem_out = ring + i if way == 1 else out_left
 
@@ -164,7 +179,7 @@
         own_sends(b, lambda c: c.start())
 
     def gather_step(b, t, arrived, act):
-        for way, depth, reach in ways:
+        for way, depth, reach in ways[b]:
             source = lax.rem(z - way * t + ring, ring)
 
             @pl.when((t < reach) & (depth < half - 1))
@@ -181,7 +196,7 @@
                 act(g_copy(b, slot, jnp.where(depth < half - 1, slot, source), slot, way))
 
     def gather_rest(b):
-        for way, depth, reach in ways:
+        for way, depth, reach in ways[b]:
 
             @pl.when(depth < half - 1)
             def _():
@@ -215,7 +230,7 @@
         return jnp.concatenate([total[:, :quarter], tail], axis=1).astype(BF16)
 
     def reduce_step(b, t):
-        for way, depth, reach in ways:
+        for way, depth, reach in ways[b]:
             dest = lax.rem(z - way * t + ring, ring)
             local, other = dest, ring + lax.rem(dest, half)
             if way == -1:
@@ -244,7 +259,7 @@
                 r_copy(b, slot, other, way).start()
 
     def reduce_drain(b, t):
-        for way, depth, reach in ways:
+        for way, depth, reach in ways[b]:
             dest = lax.rem(z - way * t + ring, ring)
 
             @pl.when(t <= reach)
@@ -322,6 +337,11 @@
             lhs[:, : hid * QUARTERS], weights, preferred_element_type=F32
         ).reshape(ring, 16, quarter)
 
+    squares = jnp.zeros((x_bwd.shape[0], 1), F32)
+    for q in range(QUARTERS):
+        piece = x_bwd[:, block(q)].astype(F32)
+        squares += jnp.sum(piece * piece, axis=1, keepdims=True)
+    inverse[...] = jnp.broadcast_to(lax.rsqrt(squares / (QUARTERS * quarter) + EPSILON), inverse.shape)
     begin(0)
     begin(1)
 
@@ -378,27 +398,83 @@
             r_arrived(b, own_left)
             parts[b][z] += sums[b][own_left].astype(F32)
 
-        r_arrived(b, ring + i)
-
-        @pl.when(i < half - 1)
+        if b == 0:
+            first, second, both = ring + i, out_left, i < half - 1
+        else:
+            first, second, both = out_left, ring + i, i > 0
+        r_arrived(b, first)
+
+        @pl.when(both)
         def _():
-            r_arrived(b, out_left)
-            added = sums[b][ring + i].astype(F32) + sums[b][out_left].astype(F32)
-            sums[b][ring + i] = rounded(b, added)
-
-        rows = jnp.concatenate([rounded(b, parts[b][z]), sums[b][ring + i]], axis=0)
+            r_arrived(b, second)
+            added = sums[b][first].astype(F32) + sums[b][second].astype(F32)
+            sums[b][first] = rounded(b, added)
+
+        rows = jnp.concatenate([rounded(b, parts[b][z]), sums[b][first]], axis=0)
         fins[b][...] = exact_pick(compact(1 - a), rows)
         b_copy(b).start()
         outs[b][a] = exact_pick(compact(a), rows)
 
+    def m_copy():
+        return pltpu.make_async_remote_copy(
+            src_ref=gain_own,
+            dst_ref=gain_came,
+            send_sem=x_send.at[4],
+            recv_sem=x_recv.at[4],
+            device_id=mirror,
+            device_id_type=MESH,
+        )
+
+    lane = lax.broadcasted_iota(jnp.int32, (1, 32), 1)
+
+    def slot_rows(b):
+        b_copy(b).wait_recv()
+        outs[b][1 - a] = backs[b][...]
+        return jnp.concatenate([outs[b][0], outs[b][1]], axis=0)
+
+    def chosen(pick, q, rows):
+        mask = jnp.where(((lane >> 1) & 3) == q, pick[...], 0.0).astype(BF16)
+        return jnp.dot(mask, rows, preferred_element_type=F32)
+
+    def end_bwd():
+        rows = slot_rows(0)
+        tail = rows[:, quarter:]
+        score_out[...] = chosen(pick_bwd, 0, tail) + chosen(pick_bwd, 2, tail)
+        scale = scale_bwd[:, 0:1]
+        factor = inverse[:, 0:1]
+        products = jnp.zeros_like(scale)
+        gain_own[...] = jnp.zeros_like(gain_own)
+        for q in range(QUARTERS):
+            grad = scale * chosen(pick_bwd, q, rows[:, :quarter])
+            xhat = x_bwd[:, block(q)].astype(F32) * factor
+            gain_own[q : q + 1, :] = jnp.sum(grad * xhat, axis=0, keepdims=True)
+            products += jnp.sum(grad * gain[:, block(q)] * xhat, axis=1, keepdims=True)
+        if pairs > 1:
+            m_copy().start()
+        average = products / (QUARTERS * quarter)
+        for q in range(QUARTERS):
+            grad = scale * chosen(pick_bwd, q, rows[:, :quarter])
+            xhat = x_bwd[:, block(q)].astype(F32) * factor
+            grad_x[:, block(q)] = (factor * (grad * gain[:, block(q)] - xhat * average)).astype(BF16)
+
+    def end_fwd():
+        rows = slot_rows(1)
+        for q in range(QUARTERS):
+            y_out[:, block(q)] = (scale_fwd[:, 0:1] * chosen(pick_fwd, q, rows)).astype(BF16)
+
     finish(0)
     finish(1)
+    end_bwd()
+    end_fwd()
     for b in range(2):
-        b_copy(b).wait_recv()
-        outs[b][1 - a] = backs[b][...]
         b_copy(b).wait_send()
         x_copy(b).wait_send()
         own_sends(b, lambda c: c.wait_send())
+    if pairs > 1:
+        m_copy().wait()
+        gain_out[...] = gain_own[...] + gain_came[...]
+    else:
+        gain_out[...] = gain_own[...] + gain_own[...]
 
     @pl.loop(1, half + 1)
     def _(t):
@@ -407,7 +483,9 @@
             reduce_drain(b, t)
 
 
-def exchange(packed_bwd, packed_fwd, saved, w_gate, w_up, w_down, ring):
+def exchange(ring, *operands):
+    packed_fwd, w_gate, x_bwd = operands[1], operands[3], operands[6]
+    tokens = x_bwd.shape[0]
     quarter = packed_fwd.shape[2]
     hid = w_gate.shape[1]
     wide = quarter + EXTRA
@@ -418,12 +496,19 @@
     return pl.pallas_call(
         functools.partial(ring_kernel, ring),
         out_shape=(
-            jax.ShapeDtypeStruct((2, 16, wide), BF16),
-            jax.ShapeDtypeStruct((2, 16, quarter), BF16),
+            jax.ShapeDtypeStruct((tokens, QUARTERS * quarter), BF16),
+            jax.ShapeDtypeStruct((tokens, QUARTERS * quarter), BF16),
+            jax.ShapeDtypeStruct((tokens, EXTRA), F32),
+            jax.ShapeDtypeStruct((8, quarter), F32),
         ),
-        in_specs=[vmem] * 6,
-        out_specs=(vmem, vmem),
+        in_specs=[vmem] * 12,
+        out_specs=(vmem,) * 4,
         scratch_shapes=[
+            pltpu.VMEM((2, 16, wide), BF16),
+            pltpu.VMEM((2, 16, quarter), BF16),
+            pltpu.VMEM((8, quarter), F32),
+            pltpu.VMEM((8, quarter), F32),
+            pltpu.VMEM((tokens, EXTRA), F32),
             pltpu.VMEM((2, ring + half, 16, quarter), BF16),
             pltpu.VMEM((2, 16, quarter), BF16),
             pltpu.VMEM((rows_all, 2 * hid), F32),
@@ -436,8 +521,8 @@
             pltpu.VMEM((16, quarter), BF16),
             pltpu.VMEM((16, wide), BF16),
             pltpu.VMEM((16, quarter), BF16),
-            pltpu.SemaphoreType.DMA((4,)),
-            pltpu.SemaphoreType.DMA((4,)),
+            pltpu.SemaphoreType.DMA((5,)),
+            pltpu.SemaphoreType.DMA((5,)),
             pltpu.SemaphoreType.DMA((2, slots)),
             pltpu.SemaphoreType.DMA((2, slots)),
             pltpu.SemaphoreType.DMA((2, slots)),
@@ -449,7 +534,7 @@
         cost_estimate=pl.CostEstimate(
             flops=24 * ring * 4 * quarter * 4 * hid, bytes_accessed=24 * quarter * hid, transcendentals=0
         ),
-    )(packed_bwd, packed_fwd, saved, w_gate, w_up, w_down)
+    )(*operands)
 
 
 def per_device(
@@ -479,23 +564,24 @@
     saved = saved_z[0].reshape(2, 2, ring, CAP, hid).transpose(0, 2, 1, 3, 4)
     saved = jnp.broadcast_to(saved.reshape(2, ring, 1, 2 * CAP, hid), (2, ring, 2, 2 * CAP, hid))
     saved = saved.reshape(2, ring * 8, hid).astype(F32)
-    back, forward = exchange(packed_bwd, packed_fwd, saved, w_gate, w_up, w_down, ring)
-    quarter = width // QUARTERS
-    per_slot = unpack_rows(forward, width)
-    y_rows = (pick_gate_f[:, None] * to_tokens(select_f, per_slot)).astype(BF16)[None]
-    score = back[:, :, quarter].reshape(2, 2, QUARTERS, CAP).astype(F32)
-    score = (score[:, :, 0] + score[:, :, 2]).reshape(experts, CAP)
-    token_score = jnp.einsum("ejt,ej->t", select_b, score, precision=lax.Precision.HIGHEST)
-    grad_picks = jnp.where(window, token_score[:, None], 0.0)[None]
-    per_slot = unpack_rows(back[:, :, :quarter], width)
-    grad_normed = pick_gate_b[:, None] * to_tokens(select_b, per_slot)
-    xhat, inverse = row_norm_values(backward_input_rows[0])
-    gain_term = jnp.sum(grad_normed * xhat, axis=0)
-    count = lax.axis_size("pp")
-    mirrored = lax.ppermute(gain_term, "pp", [(p, count - 1 - p) for p in range(count)])
-    scaled = grad_normed * gain_vector_row
-    grad_rows = inverse * (scaled - xhat * jnp.mean(scaled * xhat, axis=-1, keepdims=True))
-    return (y_rows, grad_rows.astype(BF16)[None], grad_picks, (gain_term + mirrored)[None, None])
+    y_rows, grad_rows, score, gain_sum = exchange(
+        ring,
+        packed_bwd,
+        packed_fwd,
+        saved,
+        w_gate,
+        w_up,
+        w_down,
+        backward_input_rows[0],
+        norm_gain,
+        slot_picks(select_b),
+        slot_picks(select_f),
+        jnp.broadcast_to(pick_gate_b[:, None], (pick_gate_b.shape[0], EXTRA)),
+        jnp.broadcast_to(pick_gate_f[:, None], (pick_gate_f.shape[0], EXTRA)),
+    )
+    grad_picks = jnp.where(window, score[:, 0:1], 0.0)[None]
+    gain_sum = gain_sum[:QUARTERS].reshape(1, 1, width)
+    return (y_rows[None], grad_rows[None], grad_picks, gain_sum)
 
 
 def solution(mesh):

time: 213 us -> 209 us (0.981)
  starting transfers between devices: 13 us -> 0 us
  Pallas kernels: 189 us -> 198 us
  matrix products: 4.28 us -> 1.76 us
    ppermute x1 -> x0, starting transfers between devices: 13 us -> none  [per_device(): lax.ppermute(gain_term, 'pp', [(p, count - 1 - p) for p in range(count)])]
    pallas_call x1, Pallas kernels: 189 us -> 198 us  [exchange(): pl.pallas_call(functools.partial(ring_kernel, ring), out_shape=(jax.Shape...]
    dot_general x3 -> x0, matrix products: 2.53 us -> none  [the longest x2 2.33 us: to_tokens(): jnp.einsum('ejt,ejd->td', select, per_slot.astype(F32), precision=lax.Pre...]
  transfers between devices with their start and end apart: 1 -> 0, of which waited for: 0 -> 0; matrix products, arithmetic and copies ran while one was open for 2% -> 0% of each run, Pallas kernels for 0% -> 0%
where the time goes in v3:
time: 209 us; the launch traced here: 208 us
  Pallas kernels  198 us (95%)
  other arithmetic  4.76 us (2%)
  local copies, waits for them, and re-layouts  3.13 us (1%)
    pallas_call x1, Pallas kernels, exchange(): pl.pallas_call(functools.partial(ring_kernel, ring), out_shape=(jax.Shape...  198 us

profile of v3, /device:TPU:1, one launch (start us, length us, event | category | flops | bytes accessed | tf_op | source)
XLA Modules:
  0.0 208.5 jit_solution(15517553699964248239)
XLA Ops:
  0.6 0.0 copy-start
  0.6 0.0 copy-start.2
  0.7 0.8 fusion.11
  1.4 0.7 fusion.12
  2.1 0.7 fusion.13
  2.8 0.7 fusion.14
  3.6 1.2 fusion
  4.8 0.1 fusion.9
  4.9 0.1 fusion.10
  5.1 0.1 copy.48
  5.2 0.1 copy.46
  5.3 0.1 broadcast_in_dim.33.scale_bwd
  5.3 0.1 broadcast_in_dim.34.scale_fwd
  5.4 0.0 copy-start.1
  5.4 1.3 convolution_convert_fusion
  6.8 0.1 copy.51
  6.9 0.0 copy-done
  6.9 0.2 convolution_convert_fusion.1
  7.2 0.1 copy.52
  7.3 0.0 copy-done.2
  7.4 0.1 copy.44
  7.5 0.0 copy-done.1
  7.5 0.0 copy-start.3
  7.6 198.0 %shard_map.147 = (bf16[32,7168]{1,0:T(8,128)(2,1)S(1)}, bf16[32,7168]{1,0:T(8,128)(2,1)S(1)}, f32[32,128]{1,0:T(8,128)S(1)}, f32[8,1792]{1,0:T(8,128)S(1)}) custom-call(bf16[2,16,1792]{2,1,0:T(8,128)(2,1)S(1)} %reshape.75.packed_bwd, bf16[2,16,1792]{2,1,0:T(8,128)(2,1)S(1)} %reshape.77.packed_fwd, f32[2,256,128]{2,1,0:T(8,128)S(1)} %bitcast.60, ...), custom_call_target="tpu_custom_call" | custom-call | flops 2818572288 | bytes 5505024 | tf_op jit(solution)/shard_map/pallas_call | solution.py:496
  205.6 0.1 slice_reduce_fusion
  205.7 0.0 copy-done.3
  205.7 0.6 compare_select_fusion
  206.3 0.6 reshape.80
  206.9 0.8 copy.55
  207.7 0.8 copy.56
  (17 shorter events, 0.3 us)
Async XLA Ops:
  0.6 6.3 %copy-start = (bf16[1,32,7168]{2,1,0:T(8,128)(2,1)S(1)}, bf16[1,32,7168]{2,1,0:T(8,128)(2,1)}, u32[]{:S(2)}) copy-start(bf16[1,32,7168]{2,1,0:T(8,128)(2,1)} %param.16) | copy-start | bytes 1376260
  0.6 6.7 %copy-start.2 = (bf16[1,2,128,128]{3,2,1,0:T(8,128)(2,1)S(1)}, bf16[1,2,128,128]{3,2,1,0:T(8,128)(2,1)}, u32[]{:S(2)}) copy-start(bf16[1,2,128,128]{3,2,1,0:T(8,128)(2,1)} %param.19) | copy-start | bytes 196612
  5.4 2.1 %copy-start.1 = (f32[1,7168]{1,0:T(1,128)S(1)}, f32[1,7168]{1,0:T(1,128)}, u32[]{:S(2)}) copy-start(f32[1,7168]{1,0:T(1,128)} %gain.1) | copy-start | bytes 86020
  7.5 198.1 %copy-start.3 = (s32[1,32,8]{1,2,0:T(8,128)S(1)}, s32[1,32,8]{1,2,0:T(8,128)}, u32[]{:S(2)}) copy-start(s32[1,32,8]{1,2,0:T(8,128)} %param.17) | copy-start | bytes 3076

commit v4 on v3

--- a/solution.py
+++ b/solution.py
@@ -7,7 +7,6 @@
 from jax.experimental.pallas import tpu as pltpu
 from jax.sharding import PartitionSpec as P
 
-CAP = 2
 EPSILON = 1e-06
 QUARTERS = 4
 EXTRA = 128
@@ -16,60 +15,39 @@
 BF16 = jnp.bfloat16
 
 
-def route_tables(id_rows, gate_rows, experts):
-    tokens = id_rows.shape[0]
-    window = id_rows < experts
-    labels = jnp.arange(experts, dtype=jnp.int32)
-    hit_table = jnp.any(id_rows[:, :, None] == labels[None, None, :], axis=1).astype(F32)
-    earlier = (jnp.arange(tokens)[:, None] > jnp.arange(tokens)[None, :]).astype(F32)
-    slot_rank = jnp.dot(earlier, hit_table, precision=lax.Precision.HIGHEST)
-    slot_ids = jnp.arange(CAP, dtype=F32)
-    select = hit_table.T[:, None, :] * (slot_rank.T[:, None, :] == slot_ids[None, :, None]).astype(F32)
-    pick_gate = jnp.sum(jnp.where(window, gate_rows, 0.0), axis=1)
-    return (select, pick_gate, window)
-
-
-def row_norm_values(x_rows):
-    x_float = x_rows.astype(F32)
-    inverse_root_scale = lax.rsqrt(jnp.mean(x_float * x_float, axis=-1, keepdims=True) + EPSILON)
-    return (x_float * inverse_root_scale, inverse_root_scale)
-
-
-def pack_rows(select, values):
-    packed = jnp.einsum("ejt,td->ejd", select.astype(BF16), values, preferred_element_type=F32).astype(BF16)
-    experts, slots, width = packed.shape
-    folded = packed.reshape(2, 2, slots, QUARTERS, width // QUARTERS)
-    return folded.transpose(0, 1, 3, 2, 4).reshape(2, 2 * QUARTERS * slots, width // QUARTERS)
-
-
-def slot_picks(select):
-    experts, slots, tokens = select.shape
-    picks = jnp.broadcast_to(select[:, None], (experts, QUARTERS, slots, tokens))
-    return picks.reshape(experts * QUARTERS * slots, tokens).T
-
-
 def exact_pick(chooser, rows):
     return jnp.dot(chooser, rows, preferred_element_type=F32).astype(BF16)
 
 
 def ring_kernel(
     ring,
+    x_fwd,
+    dy,
+    ids_bwd,
+    ids_fwd,
+    gates_bwd,
+    gates_fwd,
+    gain,
+    x_bwd_hbm,
+    saved_hbm,
+    w_gate_hbm,
+    w_up_hbm,
+    w_down_hbm,
+    y_out,
+    grad_x,
+    score_out,
+    gain_out,
     packed_bwd,
     packed_fwd,
+    x_bwd,
     saved,
     w_gate,
     w_up,
     w_down,
-    x_bwd,
-    gain,
     pick_bwd,
     pick_fwd,
     scale_bwd,
     scale_fwd,
-    y_out,
-    grad_x,
-    score_out,
-    gain_out,
     out_bwd,
     out_fwd,
     gain_own,
@@ -93,6 +71,7 @@
     g_recv,
     r_send,
     r_recv,
+    load,
 ):
     half = ring // 2
     pp = lax.axis_index("pp")
@@ -117,11 +96,72 @@
         ((1, i, half - 1), (-1, half - 1 - i, half)),
     )
 
+    loads = [
+        pltpu.make_async_copy(source, target, load.at[n])
+        for n, (source, target) in enumerate(
+            (
+                (x_bwd_hbm, x_bwd),
+                (saved_hbm, saved),
+                (w_down_hbm, w_down),
+                (w_gate_hbm, w_gate),
+                (w_up_hbm, w_up),
+            )
+        )
+    ]
+    for copy in loads:
+        copy.start()
+
     barrier = pltpu.get_barrier_semaphore()
     pairs = lax.axis_size("pp")
     mirror = (pairs - 1 - pp, ep)
     for device in (at(z + 1), at(z - 1), partner) + ((mirror,) if pairs > 1 else ()):
         pl.semaphore_signal(barrier, inc=1, device_id=device, device_id_type=MESH)
+    tokens = dy.shape[0]
+    nt = (((1,), (1,)), ((), ()))
+
+    def block(q):
+        return slice(q * quarter, (q + 1) * quarter)
+
+    def tables(ids, gates, pick, scale):
+        slot = lax.broadcasted_iota(jnp.int32, (32, tokens), 0)
+        hits = jnp.zeros((32, tokens), F32)
+        for k in range(ids.shape[0]):
+            hits += jnp.where(ids[k : k + 1, :] == (slot >> 3), 1.0, 0.0)
+        from_t = lax.broadcasted_iota(jnp.int32, (tokens, tokens), 0)
+        to_t = lax.broadcasted_iota(jnp.int32, (tokens, tokens), 1)
+        earlier = jnp.where(from_t < to_t, 1.0, 0.0).astype(BF16)
+        rank = jnp.dot(hits.astype(BF16), earlier, preferred_element_type=F32)
+        by_slot = jnp.where(rank == (slot & 1).astype(F32), hits, 0.0)
+        same = jnp.where(from_t == to_t, 1.0, 0.0).astype(BF16)
+        pick[...] = lax.dot_general(same, by_slot.astype(BF16), nt, preferred_element_type=F32)
+        gate = jnp.sum(jnp.where(ids[...] < 4, gates[...], 0.0), axis=0, keepdims=True)
+        rest = jnp.broadcast_to(gate, (EXTRA, tokens))
+        total = jnp.zeros((tokens, EXTRA), F32)
+        for _ in range(3):
+            high = rest.astype(BF16)
+            total += lax.dot_general(same, high, nt, preferred_element_type=F32)
+            rest = rest - high.astype(F32)
+        scale[...] = total
+        return by_slot
+
+    def pack(b, by_slot, values):
+        slot = lax.broadcasted_iota(jnp.int32, (32, 1), 0)
+        total = jnp.zeros((32, quarter), F32)
+        for q in range(QUARTERS):
+            mask = jnp.where(((slot >> 1) & 3) == q, by_slot, 0.0).astype(BF16)
+            total += jnp.dot(mask, values(q), preferred_element_type=F32)
+        packed[b][0] = total[0:16].astype(BF16)
+        packed[b][1] = total[16:32].astype(BF16)
+
+    def root_scale(rows):
+        squares = jnp.zeros((tokens, 1), F32)
+        for q in range(QUARTERS):
+            piece = rows[:, block(q)].astype(F32)
+            squares += jnp.sum(piece * piece, axis=1, keepdims=True)
+        return lax.rsqrt(squares / (QUARTERS * quarter) + EPSILON)
+
+    pack(0, tables(ids_bwd, gates_bwd, pick_bwd, scale_bwd), lambda q: dy[:, block(q)])
+
     pl.semaphore_wait(barrier, 4 if pairs > 1 else 3)
 
     def x_copy(b):
@@ -134,8 +174,14 @@
             device_id_type=MESH,
         )
 
-    for b in range(2):
-        x_copy(b).start()
+    x_copy(0).start()
+    root = root_scale(x_fwd)
+    pack(
+        1,
+        tables(ids_fwd, gates_fwd, pick_fwd, scale_fwd),
+        lambda q: (x_fwd[:, block(q)].astype(F32) * root * gain[:, block(q)]).astype(BF16),
+    )
+    x_copy(1).start()
 
     def g_copy(b, source, target, sem, way):
         return pltpu.make_async_remote_copy(
@@ -163,13 +209,13 @@
             sem_in = z if way == 1 else own_left
             sem_out = ring + i if way == 1 else out_left
 
+            @pl.when(depth >= half - reach)
+            def _():
+                act(g_copy(b, ring + i, jnp.where(depth < half - 1, ring + i, z), sem_out, way))
+
             @pl.when(depth < half - 1)
             def _():
                 act(g_copy(b, z, z, sem_in, way))
-
-            @pl.when(depth >= half - reach)
-            def _():
-                act(g_copy(b, ring + i, jnp.where(depth < half - 1, ring + i, z), sem_out, way))
 
     def begin(b):
         x_copy(b).wait_recv()
@@ -182,18 +228,18 @@
         for way, depth, reach in ways[b]:
             source = lax.rem(z - way * t + ring, ring)
 
-            @pl.when((t < reach) & (depth < half - 1))
-            def _():
-                if arrived:
-                    g_arrived(b, source)
-                act(g_copy(b, source, source, source, way))
-
             @pl.when(t <= depth - half + reach)
             def _():
                 slot = ring + i - way * t
                 if arrived:
                     g_arrived(b, slot)
                 act(g_copy(b, slot, jnp.where(depth < half - 1, slot, source), slot, way))
+
+            @pl.when((t < reach) & (depth < half - 1))
+            def _():
+                if arrived:
+                    g_arrived(b, source)
+                act(g_copy(b, source, source, source, way))
 
     def gather_rest(b):
         for way, depth, reach in ways[b]:
@@ -286,10 +332,12 @@
         tiles = value.reshape(ring, 1, 8, width)
         return jnp.concatenate([tiles, tiles], axis=1).reshape(rows_all, width)
 
-    def block(q):
-        return slice(q * quarter, (q + 1) * quarter)
-
-    nt = (((1,), (1,)), ((), ()))
+    def saved_rows(n):
+        place = lax.broadcasted_iota(jnp.int32, (ring * 8, ring * 4), 0)
+        origin = lax.broadcasted_iota(jnp.int32, (ring * 8, ring * 4), 1)
+        wanted = ((place >> 1) & 1) * (2 * ring) + (place >> 3) * 2 + (place & 1)
+        mask = jnp.where(origin == wanted, 1.0, 0.0).astype(BF16)
+        return jnp.dot(mask, saved[n], preferred_element_type=F32)
 
     def compute_bwd():
         rows = gathered[0, 0:ring].reshape(rows_all, quarter)
@@ -297,8 +345,8 @@
             piece = lax.dot_general(rows, w_down[:, block(q)], nt, preferred_element_type=F32)
             acc[:, :hid] = piece if q == 0 else jnp.where(row_quarter == q, piece, acc[:, :hid])
         grad_act = folded(acc[:, :hid])
-        pre_gate = saved[0]
-        pre_up = saved[1]
+        pre_gate = saved_rows(0)
+        pre_up = saved_rows(1)
         sig = jax.nn.sigmoid(pre_gate)
         silu = pre_gate * sig
         active = (silu * pre_up).astype(BF16).astype(F32)
@@ -337,13 +385,11 @@
             lhs[:, : hid * QUARTERS], weights, preferred_element_type=F32
         ).reshape(ring, 16, quarter)
 
-    squares = jnp.zeros((x_bwd.shape[0], 1), F32)
-    for q in range(QUARTERS):
-        piece = x_bwd[:, block(q)].astype(F32)
-        squares += jnp.sum(piece * piece, axis=1, keepdims=True)
-    inverse[...] = jnp.broadcast_to(lax.rsqrt(squares / (QUARTERS * quarter) + EPSILON), inverse.shape)
     begin(0)
     begin(1)
+    for copy in loads:
+        copy.wait()
+    inverse[...] = jnp.broadcast_to(root_scale(x_bwd), inverse.shape)
 
     def send(copy):
         copy.start()
@@ -484,9 +530,9 @@
 
 
 def exchange(ring, *operands):
-    packed_fwd, w_gate, x_bwd = operands[1], operands[3], operands[6]
-    tokens = x_bwd.shape[0]
-    quarter = packed_fwd.shape[2]
+    x_fwd, saved, w_gate, w_down = operands[0], operands[8], operands[9], operands[11]
+    tokens, width = x_fwd.shape
+    quarter = width // QUARTERS
     hid = w_gate.shape[1]
     wide = quarter + EXTRA
     half = ring // 2
@@ -501,9 +547,20 @@
             jax.ShapeDtypeStruct((tokens, EXTRA), F32),
             jax.ShapeDtypeStruct((8, quarter), F32),
         ),
-        in_specs=[vmem] * 12,
+        in_specs=[vmem] * 7 + [pl.BlockSpec(memory_space=pl.ANY)] * 5,
         out_specs=(vmem,) * 4,
         scratch_shapes=[
+            pltpu.VMEM((2, 16, quarter), BF16),
+            pltpu.VMEM((2, 16, quarter), BF16),
+            pltpu.VMEM((tokens, width), BF16),
+            pltpu.VMEM(saved.shape, BF16),
+            pltpu.VMEM(w_gate.shape, BF16),
+            pltpu.VMEM(w_gate.shape, BF16),
+            pltpu.VMEM(w_down.shape, BF16),
+            pltpu.VMEM((tokens, 32), F32),
+            pltpu.VMEM((tokens, 32), F32),
+            pltpu.VMEM((tokens, EXTRA), F32),
+            pltpu.VMEM((tokens, EXTRA), F32),
             pltpu.VMEM((2, 16, wide), BF16),
             pltpu.VMEM((2, 16, quarter), BF16),
             pltpu.VMEM((8, quarter), F32),
@@ -527,6 +584,7 @@
             pltpu.SemaphoreType.DMA((2, slots)),
             pltpu.SemaphoreType.DMA((2, slots)),
             pltpu.SemaphoreType.DMA((2, slots)),
+            pltpu.SemaphoreType.DMA((5,)),
         ],
         compiler_params=pltpu.CompilerParams(
             collective_id=0, has_side_effects=True, vmem_limit_bytes=52 * 1024 * 1024
@@ -551,33 +609,23 @@
     w_up,
     w_down,
 ):
-    experts = 4
     ring = lax.axis_size("ep") // 2
-    gain_vector_row = norm_gain[0]
     width = forward_input_rows.shape[2]
-    hid = w_gate.shape[1]
-    select_b, pick_gate_b, window = route_tables(ids_bwd[0], gate_bwd[0], experts)
-    packed_bwd = pack_rows(select_b, dy_bwd[0])
-    select_f, pick_gate_f, _ = route_tables(ids_fwd[0], gate_fwd[0], experts)
-    xhat, _ = row_norm_values(forward_input_rows[0])
-    packed_fwd = pack_rows(select_f, (xhat * gain_vector_row).astype(BF16))
-    saved = saved_z[0].reshape(2, 2, ring, CAP, hid).transpose(0, 2, 1, 3, 4)
-    saved = jnp.broadcast_to(saved.reshape(2, ring, 1, 2 * CAP, hid), (2, ring, 2, 2 * CAP, hid))
-    saved = saved.reshape(2, ring * 8, hid).astype(F32)
+    window = ids_bwd[0] < 4
     y_rows, grad_rows, score, gain_sum = exchange(
         ring,
-        packed_bwd,
-        packed_fwd,
-        saved,
+        forward_input_rows[0],
+        dy_bwd[0],
+        ids_bwd[0].T,
+        ids_fwd[0].T,
+        gate_bwd[0].T,
+        gate_fwd[0].T,
+        norm_gain,
+        backward_input_rows[0],
+        saved_z[0],
         w_gate,
         w_up,
         w_down,
-        backward_input_rows[0],
-        norm_gain,
-        slot_picks(select_b),
-        slot_picks(select_f),
-        jnp.broadcast_to(pick_gate_b[:, None], (pick_gate_b.shape[0], EXTRA)),
-        jnp.broadcast_to(pick_gate_f[:, None], (pick_gate_f.shape[0], EXTRA)),
     )
     grad_picks = jnp.where(window, score[:, 0:1], 0.0)[None]
     gain_sum = gain_sum[:QUARTERS].reshape(1, 1, width)

time: 209 us -> 205 us (0.981)
  local copies, waits for them, and re-layouts: 3.13 us -> 8.66 us
  other arithmetic: 4.76 us -> 0.6 us
  Pallas kernels: 198 us -> 195 us
    unnamed x10 -> x18, local copies, waits for them, and re-layouts: 1.56 us -> 7.89 us
    pallas_call x1, Pallas kernels: 198 us -> 195 us  [exchange(): pl.pallas_call(functools.partial(ring_kernel, ring), out_shape=(jax.Shape...]
    reduce_sum x3 -> x0, other arithmetic: 2.65 us -> none  [the longest x2 1.44 us: route_tables(): pick_gate = jnp.sum(jnp.where(window, gate_rows, 0.0), axis=1)]
where the time goes in v4:
time: 205 us
  Pallas kernels  195 us (95%)
  local copies, waits for them, and re-layouts  8.66 us (4%)
    pallas_call x1, Pallas kernels, exchange(): pl.pallas_call(functools.partial(ring_kernel, ring), out_shape=(jax.Shape...  195 us
    unnamed x18, local copies, waits for them, and re-layouts  7.89 us

profile of v4, /device:TPU:1, one launch (start us, length us, event | category | flops | bytes accessed | tf_op | source)
XLA Modules:
  0.0 204.9 jit_solution(2281791390064905774)
XLA Ops:
  0.6 0.0 copy-start
  0.6 0.7 copy-done
  1.3 0.0 copy-start.1
  1.3 1.0 copy-done.1
  2.3 0.0 copy-start.2
  2.3 1.0 copy-done.2
  3.4 0.0 copy-start.3
  3.4 0.8 copy-done.3
  4.2 0.0 copy-start.4
  4.2 0.7 copy-done.4
  5.0 0.0 copy-start.5
  5.0 0.7 copy-done.5
  5.6 0.0 copy-start.6
  5.6 0.7 copy-done.6
  6.3 0.0 copy-start.7
  6.3 0.7 copy-done.7
  7.0 195.0 %shard_map.147 = (bf16[32,7168]{1,0:T(8,128)(2,1)S(1)}, bf16[32,7168]{1,0:T(8,128)(2,1)S(1)}, f32[32,128]{1,0:T(8,128)S(1)}, f32[8,1792]{1,0:T(8,128)S(1)}) custom-call(bf16[32,7168]{1,0:T(8,128)(2,1)S(1)} %bitcast.21, bf16[32,7168]{1,0:T(8,128)(2,1)S(1)} %bitcast.22, s32[8,32]{1,0:T(8,128)S(1)} %bitcast.20, s32[8,32]{1,0:T(8,128)S(1)} %bitcast.24, ...), custom_call_target="tpu_custom_call" | custom-call | flops 2818572288 | bytes 5505024 | tf_op jit(solution)/shard_map/pallas_call | solution.py:542
  202.0 0.1 slice_reduce_fusion
  202.1 0.6 compare_select_fusion
  202.7 0.6 reshape.18
  203.4 0.8 copy.18
  204.2 0.8 copy.19
  (1 shorter events, 0.0 us)
Async XLA Ops:
  0.6 0.7 copy-start
  1.3 1.0 copy-start.1
  2.3 1.0 copy-start.2
  3.4 0.8 copy-start.3
  4.2 0.7 copy-start.4
  5.0 0.7 copy-start.5
  5.6 0.7 copy-start.6
  6.3 0.7 copy-start.7
